TPU v7x, 256 devices: a whole 4x4x8 slice. The times are simulated.
256 devices in a mesh: row: 32 (over z_lo, x, core), col: 4 (over y), depth: 2 (over z_hi).
Axes of the slice: x: 4, y: 4, z: 8 (z_hi: 2, z_lo: 4; z = z_hi * 4 + z_lo), core: 2. Of those that a mesh axis runs over, the one named last changes fastest.
Arguments:
- queries: bfloat16 [4608, 4096], P('row'), may hold values from -34 to 34, as said below
- key_states: bfloat16 [4608, 4096], P(('col', 'depth'), 'row'), may hold values from -8 to 8
- value_states: bfloat16 [4608, 4096], P(('col', 'depth'), 'row'), may hold values from -6 to 6
- grad_output: bfloat16 [4608, 4096], P('row'), may hold values from -6 to 6
- bias_table: float32 [32, 64], replicated, may hold values from -4 to 4
- gap_bucket: int32 [4608], P(('col', 'depth')), may hold values from 0 to 63
- block_order: int32 [64], replicated, may hold values from 0 to 63, as said below
Outputs:
- grad_queries: float32 [4608, 4096], P('row', ('col', 'depth'))
- grad_keys: float32 [4608, 4096], P(('col', 'depth'), 'row')
- grad_values: float32 [4608, 4096], P(('col', 'depth'), 'row')
- grad_bias: float32 [32, 64], P('row')
Inputs may be any that keep to these rules, and one draw needn't show every extreme that they name: `queries`: drawn afresh for each run; some query rows may be long and nearly aligned with a few keys. `block_order`: A permutation of the 64 blocks in which stored blocks 2 r and 2 r + 1 hold causal blocks k and 63 - k, in either order, for some k.
All inputs are finite; a program needn't handle non-finite values.
Results may differ from a plain program's by a relative error of at most 0.008.
Values may be sent and summed in bfloat16 or wider, within the bound.
A program may use at most 128 MiB of HBM per device.

v0:
```python
import jax
import jax.numpy as jnp
from jax import lax
from jax.sharding import PartitionSpec as P

masked_value = -1e30


def merged(part, axis, combine):
    gathered = jax.tree.map(lambda a: lax.all_gather(a, axis), part)

    def take(source):
        return jax.tree.map(lambda a: lax.dynamic_index_in_dim(a, source, 0, False), gathered)

    return lax.fori_loop(
        1, lax.axis_size(axis), lambda source, state: combine(state, take(source)), take(0)
    )


def causal_rows(block_order, first_row, count, block_rows):
    stored = first_row + jnp.arange(count, dtype=jnp.int32)
    return block_order[stored // block_rows] * block_rows + stored % block_rows


def pair_stats(first, second):
    joint_max = jnp.maximum(first[0], second[0])
    first_factor = jnp.exp(first[0] - joint_max)
    second_factor = jnp.exp(second[0] - joint_max)
    return (joint_max, first[1] * first_factor + second[1] * second_factor)


def attend_grads(
    query_rows, grad_rows, key_rows, value_rows, table_rows, buckets, query_pos, key_pos
):
    heads = table_rows.shape[0]
    head_dim = query_rows.shape[1] // heads
    query_heads = query_rows.reshape(query_rows.shape[0], heads, head_dim)
    grad_heads = grad_rows.reshape(grad_rows.shape[0], heads, head_dim)
    key_heads = key_rows.reshape(key_rows.shape[0], heads, head_dim)
    value_heads = value_rows.reshape(value_rows.shape[0], heads, head_dim)
    score_scale = head_dim ** (-0.5)
    levels = jnp.arange(table_rows.shape[1], dtype=jnp.int32)
    onehot = (buckets[:, None] == levels[None, :]).astype(jnp.float32)
    bias_rows = jnp.dot(table_rows, onehot.T, precision=lax.Precision.HIGHEST)
    visible = (key_pos[None, :] <= query_pos[:, None])[None]
    scores = (
        jnp.einsum("qhd,khd->hqk", query_heads, key_heads, preferred_element_type=jnp.float32)
        * score_scale
        + bias_rows[:, None, :]
    )
    scores = jnp.where(visible, scores, masked_value)
    grad_probs = jnp.einsum(
        "qhd,khd->hqk", grad_heads, value_heads, preferred_element_type=jnp.float32
    )
    local_max = jnp.max(scores, axis=2)
    weights = jnp.where(visible, jnp.exp(scores - local_max[:, :, None]), 0.0)
    local_total = jnp.sum(weights, axis=2)
    row_max, row_total = merged((local_max, local_total), ("col", "depth"), pair_stats)
    attention = weights * (jnp.exp(local_max - row_max) / row_total)[:, :, None]
    delta = lax.psum(jnp.sum(attention * grad_probs, axis=2), ("col", "depth"))
    grad_scores = attention * (grad_probs - delta[:, :, None])
    grad_low = grad_scores.astype(jnp.bfloat16)
    attention_low = attention.astype(jnp.bfloat16)
    query_term = (
        jnp.einsum("hqk,khd->qhd", grad_low, key_heads, preferred_element_type=jnp.float32).reshape(
            query_rows.shape[0], -1
        )
        * score_scale
    )
    key_term = (
        jnp.einsum(
            "hqk,qhd->khd", grad_low, query_heads, preferred_element_type=jnp.float32
        ).reshape(key_rows.shape[0], -1)
        * score_scale
    )
    value_term = jnp.einsum(
        "hqk,qhd->khd", attention_low, grad_heads, preferred_element_type=jnp.float32
    ).reshape(key_rows.shape[0], -1)
    bias_term = jnp.dot(jnp.sum(grad_scores, axis=1), onehot, precision=lax.Precision.HIGHEST)
    return (query_term, key_term, value_term, bias_term)


def per_device(queries, key_states, value_states, grad_output, bias_table, gap_bucket, block_order):
    row_count = queries.shape[0]
    block_rows = row_count // 2
    key_count = key_states.shape[0]
    key_pos = lax.axis_index(("col", "depth")) * key_count + jnp.arange(key_count, dtype=jnp.int32)
    groups = lax.axis_size("row")
    local_heads = bias_table.shape[0] // groups
    full_keys, full_values = (
        lax.all_gather(key_states, "row", axis=1, tiled=True),
        lax.all_gather(value_states, "row", axis=1, tiled=True),
    )
    query_pos = causal_rows(block_order, lax.axis_index("row") * row_count, row_count, block_rows)
    query_term, key_term, value_term, bias_term = attend_grads(
        queries, grad_output, full_keys, full_values, bias_table, gap_bucket, query_pos, key_pos
    )
    grad_queries = lax.psum_scatter(query_term, ("col", "depth"), scatter_dimension=1, tiled=True)
    grad_keys, grad_values = (
        lax.psum_scatter(key_term, "row", scatter_dimension=1, tiled=True),
        lax.psum_scatter(value_term, "row", scatter_dimension=1, tiled=True),
    )
    summed = lax.psum(bias_term, ("row", "col", "depth"))
    grad_bias = lax.dynamic_slice_in_dim(
        summed, lax.axis_index("row") * local_heads, local_heads, 0
    )
    return (grad_queries, grad_keys, grad_values, grad_bias)


def solution(mesh):
    placed = (
        P("row", None),
        P(("col", "depth"), "row"),
        P(("col", "depth"), "row"),
        P("row", None),
        P(),
        P(("col", "depth")),
        P(),
    )
    return jax.shard_map(
        per_device,
        mesh=mesh,
        in_specs=placed,
        out_specs=(
            P("row", ("col", "depth")),
            P(("col", "depth"), "row"),
            P(("col", "depth"), "row"),
            P("row", None),
        ),
        check_vma=False,
    )
```

profile of v0, /device:TPU:8, one launch (start us, length us, event | category | flops | bytes accessed | tf_op | source)
XLA Modules:
  0.0 692.0 jit_solution(9894979202716673483)
XLA Ops:
  7.2 0.7 all-gather.5.cloned.1.call-update
  7.9 0.0 all-gather.7.cloned.1.call-start
  8.0 0.7 all-gather.7.cloned.1.call-update
  8.7 0.0 reduce-scatter.4.cloned.1.call-start
  8.8 1.9 gather_fusion
  10.7 0.1 broadcast_compare_fusion
  10.8 1.1 convolution_bitcast_fusion
  11.9 73.0 %all-gather.5.cloned.1.call-done = bf16[576,4096]{1,0:T(8,128)(2,1)} async-done(((bf16[576,128]{1,0:T(8,128)(2,1)}), bf16[576,4096]{1,0:T(8,128)(2,1)}) %all-gather.5.cloned.1.call-update) | async-done | bytes 4718608 | tf_op jit(solution)/shard_map/all_gather | solution.py:91
  84.9 5.9 fusion.2
  90.8 4.4 copy-done.2
  95.2 5.0 fusion.31
  100.2 42.8 %all-gather.1 = f32[256,144]{1,0:T(8,128)S(1)} all-gather(f32[32,144]{1,0:T(8,128)S(1)} %fusion.31), channel_id=3, replica_groups=mesh['row'=32,'col'=4,'depth'=2] {'col','depth'}, dimensions={0}, use_global_device_ids=true | all-gather | bytes 165888 | tf_op jit(solution)/shard_map/all_gather | solution.py:10
  143.0 45.0 %all-gather = f32[256,144]{1,0:T(8,128)S(1)} all-gather(f32[32,144]{1,0:T(8,128)S(1)} %get-tuple-element.153), channel_id=2, replica_groups=mesh['row'=32,'col'=4,'depth'=2] {'col','depth'}, dimensions={0}, use_global_device_ids=true | all-gather | bytes 165888 | tf_op jit(solution)/shard_map/all_gather | solution.py:10
  188.0 0.4 while.17
  188.4 11.8 %multiply_reduce_fusion = (f32[32,144]{1,0:T(8,128)S(1)}, f32[32,144,576]{2,1,0:T(8,128)}) fusion(f32[32,144]{1,0:T(8,128)S(1)} %exponential_divide_fusion, f32[32,144]{1,0:T(8,128)S(1)} %get-tuple-element.153, f32[32,576]{1,0:T(8,128)S(1)} %convolution_bitcast_fusion, f32[32,144,576]{2,1,0:T(8,128)} %copy-done.2, ...), kind=kOutput, calls=%fused_computation.7 | convolution fusion | flops 700706304 | bytes 27343872 | tf_op jit(solution)/shard_map/qhd,khd->hqk/dot_general | solution.py:52
  200.3 52.9 %psum.14 = f32[32,144]{1,0:T(8,128)S(1)} all-reduce(f32[32,144]{1,0:T(8,128)S(1)} %get-tuple-element.155), channel_id=1, replica_groups=mesh['row'=32,'col'=4,'depth'=2] {'col','depth'}, use_global_device_ids=true, to_apply=%region_5.6 | all-reduce | flops 4608 | bytes 36864 | tf_op jit(solution)/shard_map/psum | solution.py:60
  253.2 10.2 %fusion.14 = (f32[32,576]{1,0:T(8,128)S(1)}, bf16[32,144,576]{2,1,0:T(8,128)(2,1)S(1)}) fusion(f32[32,144,576]{2,1,0:T(8,128)} %get-tuple-element.156, f32[32,144]{1,0:T(8,128)S(1)} %psum.14, f32[32,144]{1,0:T(8,128)S(1)} %exponential_divide_fusion, f32[32,144]{1,0:T(8,128)S(1)} %get-tuple-element.153, f32[32,576]{1,0:T(8,128)S(1)} %convolution_bitcast_fusion, ...), kind=kLoop, calls=%fused_computation.26 | loop fusion | flops 26523648 | bytes 26827776 | tf_op jit(solution)/shard_map/reduce_sum | solution.py:79
  263.4 6.6 multiply_bitcast_fusion.1
  270.0 1.6 copy.75
  271.7 0.0 reduce-scatter.8.cloned.1.call-start
  271.7 8.6 %fusion.16 = f32[32,72,8,128]{3,2,1,0:T(8,128)S(1)} fusion(f32[32,144]{1,0:T(8,128)S(1)} %exponential_divide_fusion, f32[32,144,576]{2,1,0:T(8,128)} %copy-done.2, f32[32,144]{1,0:T(8,128)S(1)} %get-tuple-element.153, f32[32,576]{1,0:T(8,128)S(1)} %convolution_bitcast_fusion, pred[144,576]{1,0:T(8,128)(4,1)S(1)} %broadcast_compare_fusion, ...), kind=kOutput, calls=%fused_computation.28 | convolution fusion | flops 698056704 | bytes 21427200 | tf_op jit(solution)/shard_map/hqk,qhd->khd/dot_general | solution.py:76
  280.3 4.9 copy.73
  285.3 0.0 reduce-scatter.6.cloned.1.call-start
  285.3 1.2 copy-done.4
  286.5 5.0 multiply_bitcast_fusion
  291.6 4.9 copy.74
  296.5 0.7 copy-done.5
  297.2 0.3 fusion.27
  297.5 78.4 %psum.15 = f32[32,64]{1,0:T(8,128)S(1)} all-reduce(f32[32,64]{1,0:T(8,128)S(1)} %fusion.27), channel_id=1, replica_groups=mesh['row'=32,'col'=4,'depth'=2] {'row','col','depth'}, use_global_device_ids=true, to_apply=%region_10.11 | all-reduce | flops 2048 | bytes 16384 | tf_op jit(solution)/shard_map/psum | solution.py:103
  375.9 0.5 constant_dynamic-slice_fusion
  376.4 150.1 %reduce-scatter.8.cloned.1.call-done = f32[576,128]{1,0:T(8,128)} async-done(((f32[576,4096]{1,0:T(8,128)}), f32[576,128]{1,0:T(8,128)}) %reduce-scatter.8.cloned.1.call-update) | async-done | bytes 294928 | tf_op jit(solution)/shard_map/reduce_scatter | solution.py:101
  526.5 158.9 %reduce-scatter.6.cloned.1.call-done = f32[576,128]{1,0:T(8,128)} async-done(((f32[576,4096]{1,0:T(8,128)}), f32[576,128]{1,0:T(8,128)}) %reduce-scatter.6.cloned.1.call-update) | async-done | bytes 294928 | tf_op jit(solution)/shard_map/reduce_scatter | solution.py:100
  (29 shorter events, 0.4 us)
Async XLA Ops:
  7.2 181.3 %copy-start = (bf16[144,4096]{1,0:T(8,128)(2,1)S(1)}, bf16[144,4096]{1,0:T(8,128)(2,1)}, u32[]{:S(2)}) copy-start(bf16[144,4096]{1,0:T(8,128)(2,1)} %param.12) | copy-start | bytes 3538948
  7.2 77.7 %all-gather.5.cloned.1.call-start = ((), (), s32[]{:S(2)}) async-start(), calls=%async_computation.3 | async-start | bytes 4866048 | tf_op jit(solution)/shard_map/all_gather | solution.py:91
  7.9 180.5 %all-gather.7.cloned.1.call-start = ((), (), s32[]{:S(2)}) async-start(), calls=%async_computation.4 | async-start | bytes 4866048 | tf_op jit(solution)/shard_map/all_gather | solution.py:92
  8.7 367.8 %reduce-scatter.4.cloned.1.call-start = ((), (), s32[]{:S(2)}) async-start(), calls=%async_computation.5 | async-start | bytes 2654208 | tf_op jit(solution)/shard_map/reduce_scatter | solution.py:98
  90.8 4.4 copy-start.2
  263.4 8.2 %copy-start.3 = (bf16[32,144,576]{2,1,0:T(8,128)(2,1)}, bf16[32,144,576]{2,1,0:T(8,128)(2,1)S(1)}, u32[]{:S(2)}) copy-start(bf16[32,144,576]{2,1,0:T(8,128)(2,1)S(1)} %get-tuple-element.152) | copy-start | bytes 15925252
  271.7 254.8 %reduce-scatter.8.cloned.1.call-start = ((), (), s32[]{:S(2)}) async-start(), calls=%async_computation.7 | async-start | bytes 9732096 | tf_op jit(solution)/shard_map/reduce_scatter | solution.py:101
  285.2 1.3 copy-start.4
  285.3 400.2 %reduce-scatter.6.cloned.1.call-start = ((), (), s32[]{:S(2)}) async-start(), calls=%async_computation.6 | async-start | bytes 9732096 | tf_op jit(solution)/shard_map/reduce_scatter | solution.py:100
  291.5 393.9 %copy-start.1 = (bf16[144,4096]{1,0:T(8,128)(2,1)S(1)}, bf16[144,4096]{1,0:T(8,128)(2,1)}, u32[]{:S(2)}) copy-start(bf16[144,4096]{1,0:T(8,128)(2,1)} %param.12) | copy-start | bytes 3538948
  296.5 0.7 copy-start.5
Sparse Core Ops, SparseCore 0:
  9.8 75.0 all-gather.4
  86.7 74.0 all-gather.6
  271.8 96.0 reduce-scatter.3
  371.1 155.4 reduce-scatter.7
  529.7 155.6 reduce-scatter.5
where the time goes:
time: 692 us
  waiting for transfers between devices  383 us (55%)
  blocking collectives  219 us (32%)
  matrix products  39.3 us (6%)
  local copies, waits for them, and re-layouts  20.2 us (3%)
  other arithmetic  15.5 us (2%)
  between operations  13.9 us (2%)
    reduce_scatter x1, waiting for transfers between devices, per_device(): lax.psum_scatter(key_term, 'row', scatter_dimension=1, tiled=True)  159 us
    reduce_scatter x1, waiting for transfers between devices, per_device(): lax.psum_scatter(value_term, 'row', scatter_dimension=1, tiled=True)  150 us
    all_gather x2, blocking collectives, merged(): gathered = jax.tree.map(lambda a: lax.all_gather(a, axis), part)  87.8 us
    psum x1, blocking collectives, per_device(): summed = lax.psum(bias_term, ('row', 'col', 'depth'))  78.4 us
    all_gather x1, waiting for transfers between devices, per_device(): lax.all_gather(key_states, 'row', axis=1, tiled=True)  73 us
    psum x1, blocking collectives, attend_grads(): delta = lax.psum(jnp.sum(attention * grad_probs, axis=2), ('col', 'depth'))  52.9 us
  transfers between devices with their start and end apart: 5, of which 3 were waited for; matrix products, arithmetic and copies ran while one was open for 6% of the time, Pallas kernels for 0%

commit v1 on v0

v1 whole, which is shorter than its diff:
```python
import functools
import math

import jax
import jax.numpy as jnp
from jax import lax
from jax.experimental import pallas as pl
from jax.experimental.pallas import tpu as pltpu
from jax.sharding import PartitionSpec as P

rows = 144
dim = 128
keys = 576
both = 2 * keys
levels = 64
slots = 16
queries = slots * rows
cuts = (0, 512, 1152, 1664, 2304)
z_steps = (0, 1, 3, 2)
tile = 384
tiles = both // tile
scale = dim ** -0.5
log2e = math.log2(math.e)
masked_value = -1e30
floor_value = -1e20
MESH = pl.DeviceIdType.MESH


def fold(a, combine):
    return combine(a.reshape(a.shape[0] // 8, 8, a.shape[1]), axis=0)


def wide(a, count):
    return jnp.concatenate([a] * count, axis=1)


def nt_dot(a, b):
    return lax.dot_general(a, b, (((1,), (1,)), ((), ())), preferred_element_type=jnp.float32)


def nn_dot(a, b):
    return jnp.dot(a, b, preferred_element_type=jnp.float32)


def column_of(row):
    pieces = []
    eye = lax.broadcasted_iota(jnp.int32, (dim, dim), 0) == lax.broadcasted_iota(
        jnp.int32, (dim, dim), 1
    )
    for start in range(0, keys, dim):
        spread = jnp.broadcast_to(row[:, start : start + dim], (dim, dim))
        column = jnp.sum(jnp.where(eye, spread, 0.0), axis=1, keepdims=True)
        pieces.append(column[: min(dim, keys - start)])
    return jnp.concatenate(pieces, axis=0)


def kernel(
    q_ref,
    g_ref,
    k_ref,
    v_ref,
    table_ref,
    gap_ref,
    order_ref,
    dq_out,
    dk_out,
    dv_out,
    db_out,
    q_all,
    g_all,
    k_all,
    v_all,
    k_turned,
    gap_own,
    gap_got,
    gap_cols,
    bias_cols,
    key_pos,
    query_pos,
    s_all,
    dp_all,
    stats,
    stats_got,
    dq_turned,
    dq_all,
    dq_got,
    dk_sum,
    dv_sum,
    ds_sum,
    dk_low,
    dv_low,
    dk_got,
    dv_got,
    db_own,
    db_got,
    kv_send,
    kv_recv,
    q_send,
    q_recv,
    g_send,
    g_recv,
    st_send,
    st_recv,
    dq_send,
    dq_recv,
    dkv_send,
    dkv_recv,
    db_send,
    db_recv,
):
    row = lax.axis_index("row")
    col = lax.axis_index("col")
    depth = lax.axis_index("depth")
    z_lo = row // 8
    x = (row // 2) % 4
    core = row % 2
    z = depth * 4 + z_lo
    member = col // 2
    other = (core + member) % 2
    partner = 3 - col
    own_row = member == 0
    dq_self = (member == 0) & (col == z_lo) & (depth == x // 2)

    def at(step, xx):
        there = (z + step + 8) % 8
        return ((there % 4) * 8 + xx * 2 + other, col, there // 4)

    def dq_target(j, xx):
        return (((z_lo + z_steps[j]) % 4) * 8 + xx * 2 + other, z_lo, x // 2)

    def peer(a, b):
        return (row, (col + a) % 4, (depth + b) % 2)

    def stat_peer(a, b):
        return (row, member * 2 + (col + a) % 2, (depth + b) % 2)

    barrier = pltpu.get_barrier_semaphore()

    def greet(device):
        pl.semaphore_signal(barrier, inc=1, device_id=device, device_id_type=MESH)

    for step in (0, 1, -1, 2, -2):

        def greet_row(i, carry, step=step):
            if step == 0:

                @pl.when(jnp.logical_not(own_row & (i == x)))
                def _():
                    greet(at(step, i))

            else:
                greet(at(step, i))
            return carry

        lax.fori_loop(0, 4, greet_row, 0)

    for n in range(1, 8):
        greet(peer(n // 2, n % 2))

    def greet_source(i, carry):
        head_x = depth * 2 + i // 8
        head_core = (i // 4) % 2
        source_col = ((head_core + core) % 2) * 2 + (i // 2) % 2
        is_self = dq_self & (head_x == x) & (head_core == core) & (source_col == col) & (
            i % 2 == depth
        )

        @pl.when(jnp.logical_not(is_self))
        def _():
            greet((col * 8 + head_x * 2 + head_core, source_col, i % 2))

        return carry

    lax.fori_loop(0, slots, greet_source, 0)

    gap_own[...] = jnp.zeros_like(gap_own)
    gap_own[0:1, 0:keys] = gap_ref[...].astype(jnp.float32)
    k_all[0:keys, :] = k_ref[...]
    v_all[0:keys, :] = v_ref[...]

    expected = 20 + 7 + 16 - own_row.astype(jnp.int32) - dq_self.astype(jnp.int32)
    pl.semaphore_wait(barrier, expected)

    mate = (row, partner, depth)
    exchange = [
        pltpu.make_async_remote_copy(
            src_ref=src,
            dst_ref=dst,
            send_sem=kv_send.at[n],
            recv_sem=kv_recv.at[n],
            device_id=mate,
            device_id_type=MESH,
        )
        for n, (src, dst) in enumerate(
            (
                (gap_own, gap_got),
                (k_ref, k_all.at[pl.ds(keys, keys), :]),
                (v_ref, v_all.at[pl.ds(keys, keys), :]),
            )
        )
    ]
    for copy in exchange:
        copy.start()

    def send_rows(src, dst, send_sem, recv_sem, step, j):
        def one(i, carry):
            xx = (x + i) % 4
            target = at(step, xx)
            src_part = src.at[:, pl.ds(pl.multiple_of(target[0] * dim, dim), dim)]
            dst_part = dst.at[pl.ds(pl.multiple_of((j * 4 + x) * rows, rows), rows), :]

            def remote():
                pltpu.make_async_remote_copy(
                    src_ref=src_part,
                    dst_ref=dst_part,
                    send_sem=send_sem,
                    recv_sem=recv_sem.at[j],
                    device_id=target,
                    device_id_type=MESH,
                ).start()

            if step == 0:
                mine = own_row & (i == 0)

                @pl.when(mine)
                def _():
                    pltpu.make_async_copy(src_part, dst_part, recv_sem.at[j]).start()

                @pl.when(jnp.logical_not(mine))
                def _():
                    remote()

            else:
                remote()
            return carry

        lax.fori_loop(0, 4, one, 0)

    for step, j in ((0, 0), (-1, 1), (1, 2)):
        send_rows(q_ref, q_all, q_send, q_recv, step, j)
        send_rows(g_ref, g_all, g_send, g_recv, step, j)
    send_rows(q_ref, q_all, q_send, q_recv, -2, 3)
    send_rows(g_ref, g_all, g_send, g_recv, 2, 3)

    lane = lax.broadcasted_iota(jnp.int32, (1, queries), 1)
    half = rows // 2

    def place(b, pos):
        slot = b // 2
        j = slot // 4
        step = j + (j // 2) * (1 - 2 * (j % 2))
        r = ((z_lo + step) % 4) * 8 + (slot % 4) * 2 + other
        first = order_ref[2 * r + b % 2] * half
        inside = (lane >= b * half) & (lane < b * half + half)
        return jnp.where(inside, first + lane - b * half, pos)

    query_pos[...] = lax.fori_loop(0, 2 * slots, place, jnp.zeros((1, queries), jnp.int32))
    block = col * 2 + depth
    partner_block = partner * 2 + depth
    within = lax.broadcasted_iota(jnp.int32, (keys, dim), 0)
    key_pos[0:keys, :] = within + block * keys
    key_pos[keys:both, :] = within + partner_block * keys
    level = lax.broadcasted_iota(jnp.int32, (1, levels), 1).astype(jnp.float32)
    table = table_ref[pl.ds(row, 1), :]

    def fill_bias(gap, start):
        column = column_of(gap)
        gap_cols[start : start + keys, :] = jnp.broadcast_to(column, (keys, dim))
        bias = jnp.sum(jnp.where(column == level, table, 0.0), axis=1, keepdims=True)
        bias_cols[start : start + keys, :] = jnp.broadcast_to(bias * log2e, (keys, dim))

    fill_bias(gap_own[0:1, :], 0)
    dk_sum[...] = jnp.zeros_like(dk_sum)
    dv_sum[...] = jnp.zeros_like(dv_sum)
    ds_sum[...] = jnp.zeros_like(ds_sum)
    for copy in exchange:
        copy.wait()
    fill_bias(gap_got[0:1, :], keys)
    for t in range(tiles):
        part = k_all[t * tile : (t + 1) * tile, :].astype(jnp.float32)
        k_turned[t] = part.T.astype(jnp.bfloat16)

    def wait_group(buffer, sem, j):
        part = buffer.at[pl.ds(j * 4 * rows, 4 * rows), :]
        pltpu.make_async_copy(part, part, sem.at[j]).wait()

    def stat_copy(c, n):
        lo, hi = cuts[c], cuts[c + 1]
        return pltpu.make_async_remote_copy(
            src_ref=stats.at[:, pl.ds(lo, hi - lo)],
            dst_ref=stats_got.at[n - 1, :, pl.ds(lo, hi - lo)],
            send_sem=st_send.at[c, n - 1],
            recv_sem=st_recv.at[c, n - 1],
            device_id=stat_peer(n // 2, n % 2),
            device_id_type=MESH,
        )

    for c in range(4):
        lo, hi = cuts[c], cuts[c + 1]
        count = hi - lo
        wait_group(q_all, q_recv, c)
        pos = query_pos[:, lo:hi]
        q_part = q_all[lo:hi, :]

        def scores(t, best):
            start = pl.multiple_of(t * tile, tile)
            part = pl.ds(start, tile)
            s = nt_dot(k_all[part, :], q_part) * (scale * log2e)
            s = s + wide(bias_cols[part, :], count // dim)
            s = jnp.where(wide(key_pos[part, :], count // dim) <= pos, s, masked_value)
            s_all[part, lo:hi] = s
            return jnp.maximum(best, fold(s, jnp.max))

        best = lax.fori_loop(0, tiles, scores, jnp.full((8, count), masked_value, jnp.float32))
        best = jnp.maximum(jnp.max(best, axis=0, keepdims=True), floor_value)
        wait_group(g_all, g_recv, c)
        g_part = g_all[lo:hi, :]

        def sums(t, state):
            start = pl.multiple_of(t * tile, tile)
            part = pl.ds(start, tile)
            dp = nt_dot(v_all[part, :], g_part)
            dp_all[part, lo:hi] = dp
            w = jnp.exp2(s_all[part, lo:hi] - best)
            return state[0] + fold(w, jnp.sum), state[1] + fold(w * dp, jnp.sum)

        zero = jnp.zeros((8, count), jnp.float32)
        total, moment = lax.fori_loop(0, tiles, sums, (zero, zero))
        stats[0:1, lo:hi] = best
        stats[1:2, lo:hi] = jnp.sum(total, axis=0, keepdims=True)
        stats[2:3, lo:hi] = jnp.sum(moment, axis=0, keepdims=True)
        for n in range(1, 4):
            stat_copy(c, n).start()

    sent = 0
    for c in range(4):
        lo, hi = cuts[c], cuts[c + 1]
        count = hi - lo
        for n in range(1, 4):
            stat_copy(c, n).wait()
        parts = [stats[0:3, lo:hi]] + [stats_got[n, 0:3, lo:hi] for n in range(3)]
        best = functools.reduce(jnp.maximum, [a[0:1] for a in parts])
        factors = [jnp.exp2(a[0:1] - best) for a in parts]
        total = sum(a[1:2] * f for a, f in zip(parts, factors))
        moment = sum(a[2:3] * f for a, f in zip(parts, factors))
        lse = best + jnp.log(total) * log2e
        delta = moment / total
        q_part = q_all[lo:hi, :]
        g_part = g_all[lo:hi, :]
        dq_turned[...] = jnp.zeros_like(dq_turned)

        def grads(t, carry):
            start = pl.multiple_of(t * tile, tile)
            part = pl.ds(start, tile)
            p = jnp.exp2(s_all[part, lo:hi] - lse)
            ds = p * (dp_all[part, lo:hi] - delta)
            ds_sum[part, :] += sum(
                ds[:, n * dim : (n + 1) * dim] for n in range(count // dim)
            )
            ds_low = ds.astype(jnp.bfloat16)
            dv_sum[part, :] += nn_dot(p.astype(jnp.bfloat16), g_part)
            dk_sum[part, :] += nn_dot(ds_low, q_part)
            dq_turned[:, 0:count] += nn_dot(k_turned[t], ds_low)
            return carry

        lax.fori_loop(0, tiles, grads, 0)
        dq_all[lo:hi, :] = (dq_turned[:, 0:count].T * scale).astype(jnp.bfloat16)
        while (sent + 1) * rows <= hi:
            j, xx = sent // 4, sent % 4
            src = dq_all.at[pl.ds(sent * rows, rows), :]
            place_at = ((x % 2) * 2 + core) * 4 + (col % 2) * 2 + depth
            dst = dq_got.at[place_at]

            def remote(j=j, xx=xx, src=src):
                pltpu.make_async_remote_copy(
                    src_ref=src,
                    dst_ref=dst,
                    send_sem=dq_send,
                    recv_sem=dq_recv,
                    device_id=dq_target(j, xx),
                    device_id_type=MESH,
                ).start()

            if j == 0:
                mine = dq_self & (x == xx)

                @pl.when(mine)
                def _(src=src):
                    pltpu.make_async_copy(src, dst, dq_recv).start()

                @pl.when(jnp.logical_not(mine))
                def _(remote=remote):
                    remote()

            else:
                remote()
            sent += 1

    dk_low[...] = (dk_sum[keys:both, :] * scale).astype(jnp.bfloat16)
    dv_low[...] = dv_sum[keys:both, :].astype(jnp.bfloat16)
    returns = [
        pltpu.make_async_remote_copy(
            src_ref=src,
            dst_ref=dst,
            send_sem=dkv_send.at[n],
            recv_sem=dkv_recv.at[n],
            device_id=mate,
            device_id_type=MESH,
        )
        for n, (src, dst) in enumerate(((dk_low, dk_got), (dv_low, dv_got)))
    ]
    for copy in returns:
        copy.start()

    column = jnp.sum(ds_sum[...], axis=1, keepdims=True)
    by_level = jnp.where(gap_cols[:, 0:levels] == level, column, 0.0)
    db_own[...] = jnp.zeros_like(db_own)
    db_own[0:1, 0:levels] = jnp.sum(by_level, axis=0, keepdims=True)
    biases = [
        pltpu.make_async_remote_copy(
            src_ref=db_own,
            dst_ref=db_got.at[n - 1],
            send_sem=db_send.at[n - 1],
            recv_sem=db_recv.at[n - 1],
            device_id=peer(n // 2, n % 2),
            device_id_type=MESH,
        )
        for n in range(1, 8)
    ]
    for copy in biases:
        copy.start()

    for copy in returns:
        copy.wait()
    dk_out[...] = dk_sum[0:keys, :] * scale + dk_got[...].astype(jnp.float32)
    dv_out[...] = dv_sum[0:keys, :] + dv_got[...].astype(jnp.float32)
    for copy in biases:
        copy.wait()
    db_out[...] = db_own[0:1, 0:levels] + sum(db_got[n, 0:1, 0:levels] for n in range(7))

    pltpu.make_async_copy(dq_got, dq_got, dq_recv).wait()
    for head in range(4):
        dq_out[:, head * dim : (head + 1) * dim] = sum(
            dq_got[head * 4 + n].astype(jnp.float32) for n in range(4)
        )

    def drain(buffer, sem, short):
        @pl.when(short)
        def _():
            part = buffer.at[pl.ds(0, queries - rows), :]
            pltpu.make_async_copy(part, part, sem).wait()

        @pl.when(jnp.logical_not(short))
        def _():
            pltpu.make_async_copy(buffer, buffer, sem).wait()

    drain(q_all, q_send, own_row)
    drain(g_all, g_send, own_row)
    drain(dq_all, dq_send, dq_self)


def per_device(queries_in, key_states, value_states, grad_output, bias_table, gap_bucket, order):
    vmem = pl.BlockSpec(memory_space=pltpu.VMEM)
    anywhere = pl.BlockSpec(memory_space=pl.ANY)
    low, full = jnp.bfloat16, jnp.float32
    dma = pltpu.SemaphoreType.DMA
    return pl.pallas_call(
        kernel,
        out_shape=(
            jax.ShapeDtypeStruct((rows, 4 * dim), full),
            jax.ShapeDtypeStruct((keys, dim), full),
            jax.ShapeDtypeStruct((keys, dim), full),
            jax.ShapeDtypeStruct((1, levels), full),
        ),
        in_specs=[
            anywhere,
            anywhere,
            vmem,
            vmem,
            vmem,
            vmem,
            pl.BlockSpec(memory_space=pltpu.SMEM),
        ],
        out_specs=(vmem, vmem, vmem, vmem),
        scratch_shapes=[
            pltpu.VMEM((queries, dim), low),
            pltpu.VMEM((queries, dim), low),
            pltpu.VMEM((both, dim), low),
            pltpu.VMEM((both, dim), low),
            pltpu.VMEM((tiles, dim, tile), low),
            pltpu.VMEM((8, 640), full),
            pltpu.VMEM((8, 640), full),
            pltpu.VMEM((both, dim), full),
            pltpu.VMEM((both, dim), full),
            pltpu.VMEM((both, dim), jnp.int32),
            pltpu.VMEM((1, queries), jnp.int32),
            pltpu.VMEM((both, queries), full),
            pltpu.VMEM((both, queries), full),
            pltpu.VMEM((8, queries), full),
            pltpu.VMEM((3, 8, queries), full),
            pltpu.VMEM((dim, 640), full),
            pltpu.VMEM((queries, dim), low),
            pltpu.VMEM((slots, rows, dim), low),
            pltpu.VMEM((both, dim), full),
            pltpu.VMEM((both, dim), full),
            pltpu.VMEM((both, dim), full),
            pltpu.VMEM((keys, dim), low),
            pltpu.VMEM((keys, dim), low),
            pltpu.VMEM((keys, dim), low),
            pltpu.VMEM((keys, dim), low),
            pltpu.VMEM((8, dim), full),
            pltpu.VMEM((7, 8, dim), full),
            dma((3,)),
            dma((3,)),
            dma(()),
            dma((4,)),
            dma(()),
            dma((4,)),
            dma((4, 3)),
            dma((4, 3)),
            dma(()),
            dma(()),
            dma((2,)),
            dma((2,)),
            dma((7,)),
            dma((7,)),
        ],
        compiler_params=pltpu.CompilerParams(
            collective_id=0, has_side_effects=True, vmem_limit_bytes=48 * 1024 * 1024
        ),
        cost_estimate=pl.CostEstimate(
            flops=10 * both * queries * dim,
            bytes_accessed=8 * queries * dim,
            transcendentals=2 * both * queries,
        ),
    )(
        queries_in,
        grad_output,
        key_states,
        value_states,
        bias_table,
        gap_bucket.reshape(1, keys),
        order,
    )


def solution(mesh):
    placed = (
        P("row", None),
        P(("col", "depth"), "row"),
        P(("col", "depth"), "row"),
        P("row", None),
        P(),
        P(("col", "depth")),
        P(),
    )
    return jax.shard_map(
        per_device,
        mesh=mesh,
        in_specs=placed,
        out_specs=(
            P("row", ("col", "depth")),
            P(("col", "depth"), "row"),
            P(("col", "depth"), "row"),
            P("row", None),
        ),
        check_vma=False,
    )
```

time: 692 us -> 74.7 us (0.11)
  the two profiles are of different devices: /device:TPU:8 before, /device:TPU:71 now
where the time goes in v1:
time: 74.7 us; the launch traced here: 74.4 us
  Pallas kernels  64.7 us (87%)
  local copies, waits for them, and re-layouts  9.07 us (12%)
    pallas_call x1, Pallas kernels, per_device(): pl.pallas_call(kernel, out_shape=(jax.ShapeDtypeStruct((rows, 4 * dim), f...  64.7 us
    unnamed x16, local copies, waits for them, and re-layouts  8.38 us

profile of v1, /device:TPU:71, one launch (start us, length us, event | category | flops | bytes accessed | tf_op | source)
XLA Modules:
  0.0 74.4 jit_solution(18372798625204658332)
XLA Ops:
  0.6 0.7 reshape.11.gap_ref
  1.3 0.0 copy-start
  1.3 1.3 %copy-done = bf16[144,4096]{1,0:T(8,128)(2,1)S(1)} copy-done((bf16[144,4096]{1,0:T(8,128)(2,1)S(1)}, bf16[144,4096]{1,0:T(8,128)(2,1)}, u32[]{:S(2)}) %copy-start) | copy-done | bytes 1179672
  2.6 0.0 copy-start.1
  2.6 1.3 %copy-done.1 = bf16[144,4096]{1,0:T(8,128)(2,1)S(1)} copy-done((bf16[144,4096]{1,0:T(8,128)(2,1)S(1)}, bf16[144,4096]{1,0:T(8,128)(2,1)}, u32[]{:S(2)}) %copy-start.1) | copy-done | bytes 1179672
  3.9 0.0 copy-start.2
  3.9 0.9 %copy-done.2 = bf16[576,128]{1,0:T(8,128)(2,1)S(1)} copy-done((bf16[576,128]{1,0:T(8,128)(2,1)S(1)}, bf16[576,128]{1,0:T(8,128)(2,1)}, u32[]{:S(2)}) %copy-start.2) | copy-done | bytes 147480
  4.8 0.0 copy-start.3
  4.8 0.9 %copy-done.3 = bf16[576,128]{1,0:T(8,128)(2,1)S(1)} copy-done((bf16[576,128]{1,0:T(8,128)(2,1)S(1)}, bf16[576,128]{1,0:T(8,128)(2,1)}, u32[]{:S(2)}) %copy-start.3) | copy-done | bytes 147480
  5.7 0.0 copy-start.4
  5.7 0.7 copy-done.4
  6.4 0.0 copy-start.5
  6.4 0.7 copy-done.5
  7.1 64.7 %shard_map.102 = (f32[144,512]{1,0:T(8,128)S(1)}, f32[576,128]{1,0:T(8,128)S(1)}, f32[576,128]{1,0:T(8,128)S(1)}, f32[1,64]{1,0:T(1,128)S(1)}) custom-call(bf16[144,4096]{1,0:T(8,128)(2,1)S(1)} %copy-done, bf16[144,4096]{1,0:T(8,128)(2,1)S(1)} %copy-done.1, bf16[576,128]{1,0:T(8,128)(2,1)S(1)} %copy-done.2, bf16[576,128]{1,0:T(8,128)(2,1)S(1)} %copy-done.3, ...), custom_call_target="tpu_custom_call" | custom-call | flops 3397386240 | bytes 2359296 | tf_op jit(solution)/shard_map/pallas_call | solution.py:467
  71.7 0.7 copy.15
  72.4 0.7 copy.16
  73.2 0.7 copy.17
  73.9 0.5 copy.18
Async XLA Ops:
  1.3 1.3 %copy-start = (bf16[144,4096]{1,0:T(8,128)(2,1)S(1)}, bf16[144,4096]{1,0:T(8,128)(2,1)}, u32[]{:S(2)}) copy-start(bf16[144,4096]{1,0:T(8,128)(2,1)} %q_ref.1) | copy-start | bytes 3538948
  2.6 1.3 %copy-start.1 = (bf16[144,4096]{1,0:T(8,128)(2,1)S(1)}, bf16[144,4096]{1,0:T(8,128)(2,1)}, u32[]{:S(2)}) copy-start(bf16[144,4096]{1,0:T(8,128)(2,1)} %g_ref.1) | copy-start | bytes 3538948
  3.9 0.9 %copy-start.2 = (bf16[576,128]{1,0:T(8,128)(2,1)S(1)}, bf16[576,128]{1,0:T(8,128)(2,1)}, u32[]{:S(2)}) copy-start(bf16[576,128]{1,0:T(8,128)(2,1)} %k_ref.1) | copy-start | bytes 442372
  4.8 0.9 %copy-start.3 = (bf16[576,128]{1,0:T(8,128)(2,1)S(1)}, bf16[576,128]{1,0:T(8,128)(2,1)}, u32[]{:S(2)}) copy-start(bf16[576,128]{1,0:T(8,128)(2,1)} %v_ref.1) | copy-start | bytes 442372
  5.7 0.7 copy-start.4
  6.4 0.7 copy-start.5

commit v2 on v1

v2 whole, which is shorter than its diff:
```python
import functools
import math

import jax
import jax.numpy as jnp
from jax import lax
from jax.experimental import pallas as pl
from jax.experimental.pallas import tpu as pltpu
from jax.sharding import PartitionSpec as P

rows = 144
dim = 128
keys = 576
blocks = 4
all_keys = blocks * keys
levels = 64
slots = 8
queries = slots * rows
chunk = 384
chunks = queries // chunk
z_steps = (0, 1, 3, 2)
tile = 288
per_block = keys // tile
tiles = blocks * per_block
scale = dim ** -0.5
log2e = math.log2(math.e)
masked_value = -1e30
floor_value = -1e20
MESH = pl.DeviceIdType.MESH


def fold(a, combine):
    return combine(a.reshape(a.shape[0] // 8, 8, a.shape[1]), axis=0)


def wide(a):
    return jnp.concatenate([a] * (chunk // dim), axis=1)


def nt_dot(a, b):
    return lax.dot_general(a, b, (((1,), (1,)), ((), ())), preferred_element_type=jnp.float32)


def nn_dot(a, b):
    return jnp.dot(a, b, preferred_element_type=jnp.float32)


def column_of(row):
    pieces = []
    eye = lax.broadcasted_iota(jnp.int32, (dim, dim), 0) == lax.broadcasted_iota(
        jnp.int32, (dim, dim), 1
    )
    for start in range(0, keys, dim):
        spread = jnp.broadcast_to(row[:, start : start + dim], (dim, dim))
        column = jnp.sum(jnp.where(eye, spread, 0.0), axis=1, keepdims=True)
        pieces.append(column[: min(dim, keys - start)])
    return jnp.concatenate(pieces, axis=0)


def merge(parts):
    best = functools.reduce(jnp.maximum, [a[0:1] for a in parts])
    factors = [jnp.exp2(a[0:1] - best) for a in parts]
    total = sum(a[1:2] * f for a, f in zip(parts, factors))
    moment = sum(a[2:3] * f for a, f in zip(parts, factors))
    return best, total, moment


def kernel(
    q_ref,
    g_ref,
    k_ref,
    v_ref,
    table_ref,
    gap_ref,
    order_ref,
    dq_out,
    dk_out,
    dv_out,
    db_out,
    q_all,
    g_all,
    k_all,
    v_all,
    k_turned,
    gap_rows,
    gap_cols,
    bias_cols,
    key_pos,
    query_pos,
    s_all,
    dp_all,
    part_stats,
    stats,
    stats_got,
    dq_turned,
    dq_all,
    mid_got,
    mid_low,
    fin_got,
    dk_sum,
    dv_sum,
    ds_sum,
    kv_low,
    kv_got,
    db_own,
    db_got,
    local_sem,
    gap_send,
    gap_recv,
    k_send,
    k_recv,
    v_send,
    v_recv,
    q_send,
    q_recv,
    g_send,
    g_recv,
    st_send,
    st_recv,
    dq_send,
    dq_recv,
    fin_send,
    fin_recv,
    dkv_send,
    dkv_recv,
    db_send,
    db_recv,
):
    row = lax.axis_index("row")
    col = lax.axis_index("col")
    depth = lax.axis_index("depth")
    z_lo = row // 8
    x = (row // 2) % 4
    core = row % 2
    z = depth * 4 + z_lo
    member = col // 2
    parity = col % 2
    other = (core + member) % 2
    own_row = col == 0
    mid_self = (col == 0) & (depth == x // 2)

    def shift(j):
        return (parity + (1 if j in (1, 2) else 0)) % 2

    def at(step, xx):
        there = (z + step + 8) % 8
        return ((there % 4) * 8 + xx * 2 + other, col, there // 4)

    def slot_x(s):
        return (x + shift(s // 2) + 2 * (s % 2)) % 4

    def peer(a, b):
        return (row, (col + a) % 4, (depth + b) % 2)

    barrier = pltpu.get_barrier_semaphore()

    def greet(device):
        pl.semaphore_signal(barrier, inc=1, device_id=device, device_id_type=MESH)

    for step, j in ((0, 0), (1, 1), (-1, 2), (2, 3), (-2, 3)):
        for i in range(2):
            device = at(step, (x + shift(j) + 2 * i) % 4)
            if step == 0 and i == 0:

                @pl.when(jnp.logical_not(own_row))
                def _(device=device):
                    greet(device)

            else:
                greet(device)
    for n in range(1, 8):
        greet(peer(n // 2, n % 2))
    for n in range(8):
        head_z, head_depth = n // 2, n % 2
        head_x = depth * 2 + (x + z_lo + 4 - head_z + parity) % 2

        @pl.when(jnp.logical_not(mid_self & (z_lo == head_z) & (depth == head_depth)))
        def _(head_z=head_z, head_depth=head_depth, head_x=head_x):
            greet((head_z * 8 + head_x * 2 + other, col, head_depth))

    own_k = pltpu.make_async_copy(k_ref, k_all.at[0], local_sem.at[0])
    own_v = pltpu.make_async_copy(v_ref, v_all.at[0], local_sem.at[1])
    own_k.start()
    own_v.start()
    gap_rows[0] = jnp.zeros((8, 640), jnp.float32)
    gap_rows[0, 0:1, 0:keys] = gap_ref[...].astype(jnp.float32).reshape(1, keys)

    pl.semaphore_wait(
        barrier, 25 - own_row.astype(jnp.int32) - mid_self.astype(jnp.int32)
    )

    def remote(src, dst, send_sem, recv_sem, device):
        return pltpu.make_async_remote_copy(
            src_ref=src,
            dst_ref=dst,
            send_sem=send_sem,
            recv_sem=recv_sem,
            device_id=device,
            device_id_type=MESH,
        )

    def gap_copy(a):
        return remote(
            gap_rows.at[0], gap_rows.at[4 - a], gap_send.at[a - 1], gap_recv.at[3 - a], peer(a, 0)
        )

    def own_copy(a, src, dst, send, recv):
        return remote(src, dst.at[4 - a], send.at[a - 1], recv.at[3 - a], peer(a, 0))

    def pass_copy(a, dst, send, recv):
        return remote(dst.at[4 - a], dst.at[2], send.at[1], recv.at[1], peer(a, 0))

    gaps = [gap_copy(a) for a in (1, 3, 2)]
    sides = [own_copy(a, k_ref, k_all, k_send, k_recv) for a in (1, 3)] + [
        own_copy(a, v_ref, v_all, v_send, v_recv) for a in (3, 1)
    ]
    k_pass = pass_copy(1, k_all, k_send, k_recv)
    v_pass = pass_copy(3, v_all, v_send, v_recv)
    for copy in (sides[0], sides[2]):
        copy.start()

    def send_rows(src, dst, send_sem, recv_sem, step, j):
        for i in range(2):
            target = at(step, (x + 3 * shift(j) + 2 * i) % 4)
            src_part = src.at[:, pl.ds(pl.multiple_of(target[0] * dim, dim), dim)]
            dst_part = dst.at[pl.ds((j * 2 + i) * rows, rows), :]
            away = remote(src_part, dst_part, send_sem, recv_sem.at[j], target)
            if step == 0 and i == 0:

                @pl.when(own_row)
                def _(src_part=src_part, dst_part=dst_part):
                    pltpu.make_async_copy(src_part, dst_part, recv_sem.at[j]).start()

                @pl.when(jnp.logical_not(own_row))
                def _(away=away):
                    away.start()

            else:
                away.start()

    send_rows(q_ref, q_all, q_send, q_recv, 0, 0)
    send_rows(g_ref, g_all, g_send, g_recv, 0, 0)
    for copy in gaps:
        copy.start()
    send_rows(q_ref, q_all, q_send, q_recv, -1, 1)
    send_rows(q_ref, q_all, q_send, q_recv, 1, 2)
    send_rows(q_ref, q_all, q_send, q_recv, -2, 3)
    send_rows(g_ref, g_all, g_send, g_recv, -1, 1)
    send_rows(g_ref, g_all, g_send, g_recv, 1, 2)
    send_rows(g_ref, g_all, g_send, g_recv, 2, 3)
    for copy in (sides[1], sides[3]):
        copy.start()

    lane = lax.broadcasted_iota(jnp.int32, (1, queries), 1)
    half = rows // 2
    pos = jnp.zeros((1, queries), jnp.int32)
    for s in range(slots):
        r = ((z_lo + z_steps[s // 2]) % 4) * 8 + slot_x(s) * 2 + other
        for b in range(2):
            low = s * rows + b * half
            inside = (lane >= low) & (lane < low + half)
            pos = jnp.where(inside, order_ref[2 * r + b] * half + lane - low, pos)
    query_pos[...] = pos
    within = lax.broadcasted_iota(jnp.int32, (keys, dim), 0)
    for b in range(blocks):
        key_pos[b * keys : (b + 1) * keys, :] = within + (((col + b) % 4) * 2 + depth) * keys
    level = lax.broadcasted_iota(jnp.int32, (1, levels), 1).astype(jnp.float32)
    table = table_ref[pl.ds(row, 1), :]

    def fill_bias(b):
        start = b * keys
        column = column_of(gap_rows[b, 0:1, :])
        gap_cols[start : start + keys, :] = jnp.broadcast_to(column, (keys, dim))
        bias = jnp.sum(jnp.where(column == level, table, 0.0), axis=1, keepdims=True)
        bias_cols[start : start + keys, :] = jnp.broadcast_to(bias * log2e, (keys, dim))

    def turn(b):
        for t in range(per_block):
            part = k_all[b, t * tile : (t + 1) * tile, :].astype(jnp.float32)
            k_turned[b * per_block + t] = part.T.astype(jnp.bfloat16)

    fill_bias(0)
    dk_sum[...] = jnp.zeros_like(dk_sum)
    dv_sum[...] = jnp.zeros_like(dv_sum)
    ds_sum[...] = jnp.zeros_like(ds_sum)
    own_k.wait()
    own_v.wait()
    turn(0)

    sides[0].wait_recv()
    k_pass.start()
    sides[2].wait_recv()
    v_pass.start()

    def wait_group(buffer, sem, j):
        part = buffer.at[pl.ds(j * 2 * rows, 2 * rows), :]
        pltpu.make_async_copy(part, part, sem.at[j]).wait()

    def first_pass(c, b):
        lo, hi = c * chunk, (c + 1) * chunk
        pos = query_pos[:, lo:hi]
        q_part = q_all[lo:hi, :]
        g_part = g_all[lo:hi, :]

        def scores(t, best):
            start = pl.multiple_of(t * tile, tile)
            part = pl.ds(pl.multiple_of(b * keys + start, tile), tile)
            s = nt_dot(k_all[b, pl.ds(start, tile), :], q_part) * (scale * log2e)
            s = s + wide(bias_cols[part, :])
            s = jnp.where(wide(key_pos[part, :]) <= pos, s, masked_value)
            s_all[part, lo:hi] = s
            return jnp.maximum(best, fold(s, jnp.max))

        best = lax.fori_loop(0, per_block, scores, jnp.full((8, chunk), masked_value, jnp.float32))
        best = jnp.maximum(jnp.max(best, axis=0, keepdims=True), floor_value)

        def sums(t, state):
            start = pl.multiple_of(t * tile, tile)
            part = pl.ds(pl.multiple_of(b * keys + start, tile), tile)
            dp = nt_dot(v_all[b, pl.ds(start, tile), :], g_part)
            dp_all[part, lo:hi] = dp
            w = jnp.exp2(s_all[part, lo:hi] - best)
            return state[0] + fold(w, jnp.sum), state[1] + fold(w * dp, jnp.sum)

        zero = jnp.zeros((8, chunk), jnp.float32)
        total, moment = lax.fori_loop(0, per_block, sums, (zero, zero))
        part_stats[b, 0:1, lo:hi] = best
        part_stats[b, 1:2, lo:hi] = jnp.sum(total, axis=0, keepdims=True)
        part_stats[b, 2:3, lo:hi] = jnp.sum(moment, axis=0, keepdims=True)

    def stat_copy(c):
        part = pl.ds(c * chunk, chunk)
        return remote(
            stats.at[:, part], stats_got.at[:, part], st_send.at[c], st_recv.at[c], peer(0, 1)
        )

    wait_group(q_all, q_recv, 0)
    wait_group(g_all, g_recv, 0)
    wait_group(q_all, q_recv, 1)
    wait_group(g_all, g_recv, 1)
    first_pass(0, 0)
    for copy in gaps:
        copy.wait_recv()
    for b in (3, 1, 2):
        fill_bias(b)
    sides[1].wait_recv()
    sides[3].wait_recv()
    turn(1)
    turn(3)
    first_pass(0, 1)
    first_pass(0, 3)
    for c in range(1, chunks):
        wait_group(q_all, q_recv, c + 1)
        wait_group(g_all, g_recv, c + 1)

        def near(i, carry, c=c):
            first_pass(c, i + i // 2)
            return carry

        lax.fori_loop(0, 3, near, 0)
    k_pass.wait_recv()
    v_pass.wait_recv()
    turn(2)
    for c in range(chunks):
        lo, hi = c * chunk, (c + 1) * chunk
        first_pass(c, 2)
        best, total, moment = merge([part_stats[b, 0:3, lo:hi] for b in range(blocks)])
        stats[0:1, lo:hi] = best
        stats[1:2, lo:hi] = total
        stats[2:3, lo:hi] = moment
        stat_copy(c).start()

    def kv_copy(n, a):
        return remote(
            kv_low.at[n], kv_got.at[n], dkv_send.at[n], dkv_recv.at[n], peer(a, 0)
        )

    returns = [kv_copy(n, a) for n, a in enumerate((1, 3, 3, 1, 1, 3))]

    def low(total, b, factor):
        return (total[b * keys : (b + 1) * keys, :] * factor).astype(jnp.bfloat16)

    sent = 0
    for c in range(chunks):
        lo, hi = c * chunk, (c + 1) * chunk
        stat_copy(c).wait()
        best, total, moment = merge([stats[0:3, lo:hi], stats_got[0:3, lo:hi]])
        lse = best + jnp.log(total) * log2e
        delta = moment / total
        q_part = q_all[lo:hi, :]
        g_part = g_all[lo:hi, :]
        dq_turned[...] = jnp.zeros_like(dq_turned)

        def grads(t, carry):
            start = pl.multiple_of(t * tile, tile)
            part = pl.ds(start, tile)
            p = jnp.exp2(s_all[part, lo:hi] - lse)
            ds = p * (dp_all[part, lo:hi] - delta)
            ds_sum[part, :] += sum(ds[:, n * dim : (n + 1) * dim] for n in range(chunk // dim))
            ds_low = ds.astype(jnp.bfloat16)
            dv_sum[part, :] += nn_dot(p.astype(jnp.bfloat16), g_part)
            dk_sum[part, :] += nn_dot(ds_low, q_part)
            dq_turned[...] += nn_dot(k_turned[t], ds_low)
            return carry

        if c < chunks - 1:
            lax.fori_loop(0, tiles, grads, 0)
        else:
            lax.fori_loop(2 * per_block, 3 * per_block, grads, 0)
            kv_low[0] = low(dk_sum, 2, scale)
            returns[0].start()
            kv_low[1] = low(dv_sum, 2, 1.0)
            returns[1].start()
            lax.fori_loop(3 * per_block, 4 * per_block, grads, 0)
            kv_low[2] = low(dk_sum, 3, scale)
            returns[2].start()
            lax.fori_loop(per_block, 2 * per_block, grads, 0)
            kv_low[3] = low(dv_sum, 1, 1.0)
            returns[3].start()
            lax.fori_loop(0, per_block, grads, 0)
        dq_all[lo:hi, :] = (dq_turned[...].T * scale).astype(jnp.bfloat16)
        while (sent + 1) * rows <= hi:
            j = sent // 2
            src = dq_all.at[pl.ds(sent * rows, rows), :]
            dst = mid_got.at[z_lo, pl.ds(pl.multiple_of(depth * rows, rows), rows), :]
            target = ((((z_lo + z_steps[j]) % 4) * 8 + slot_x(sent) * 2 + other), col, x // 2)
            away = remote(src, dst, dq_send, dq_recv.at[z_lo], target)
            if sent == 0:

                @pl.when(mid_self)
                def _(src=src, dst=dst):
                    pltpu.make_async_copy(src, dst, dq_recv.at[z_lo]).start()

                @pl.when(jnp.logical_not(mid_self))
                def _(away=away):
                    away.start()

            else:
                away.start()
            sent += 1

    column = jnp.sum(ds_sum[...], axis=1, keepdims=True)
    by_level = jnp.where(gap_cols[:, 0:levels] == level, column, 0.0)
    db_own[...] = jnp.zeros_like(db_own)
    db_own[0:1, 0:levels] = jnp.sum(by_level, axis=0, keepdims=True)
    biases = [
        remote(db_own, db_got.at[n - 1], db_send.at[n - 1], db_recv.at[n - 1], peer(n // 2, n % 2))
        for n in range(1, 8)
    ]
    for copy in biases:
        copy.start()

    returns[0].wait_recv()
    kv_low[4] = (dk_sum[keys : 2 * keys, :] * scale + kv_got[0].astype(jnp.float32)).astype(
        jnp.bfloat16
    )
    returns[4].start()
    returns[1].wait_recv()
    kv_low[5] = (dv_sum[3 * keys : 4 * keys, :] + kv_got[1].astype(jnp.float32)).astype(
        jnp.bfloat16
    )
    returns[5].start()

    def fin_copy(head_z, place):
        return remote(
            mid_low.at[head_z],
            fin_got.at[place],
            fin_send.at[head_z],
            fin_recv,
            (row, head_z, depth),
        )

    def place_of(head_z):
        return ((x + z_lo + 4 - head_z + parity) % 2) * 2 + other

    for head_z in range(4):
        both = mid_got.at[head_z]
        pltpu.make_async_copy(both, both, dq_recv.at[head_z]).wait()
        total = both[0:rows, :].astype(jnp.float32) + both[rows : 2 * rows, :].astype(jnp.float32)
        mid_low[head_z] = total.astype(jnp.bfloat16)

        @pl.when(head_z != col)
        def _(head_z=head_z):
            fin_copy(head_z, place_of(head_z)).start()

        @pl.when(head_z == col)
        def _(head_z=head_z):
            pltpu.make_async_copy(
                mid_low.at[head_z], fin_got.at[place_of(head_z)], fin_recv
            ).start()

    returns[2].wait_recv()
    returns[4].wait_recv()
    dk_out[...] = (
        dk_sum[0:keys, :] * scale + kv_got[2].astype(jnp.float32) + kv_got[4].astype(jnp.float32)
    )
    returns[3].wait_recv()
    returns[5].wait_recv()
    dv_out[...] = (
        dv_sum[0:keys, :] + kv_got[3].astype(jnp.float32) + kv_got[5].astype(jnp.float32)
    )
    for copy in biases:
        copy.wait()
    db_out[...] = db_own[0:1, 0:levels] + sum(db_got[n, 0:1, 0:levels] for n in range(7))

    pltpu.make_async_copy(fin_got, fin_got, fin_recv).wait()
    for head in range(4):
        dq_out[:, head * dim : (head + 1) * dim] = fin_got[head].astype(jnp.float32)

    def drain(buffer, sem, short):
        @pl.when(short)
        def _():
            part = buffer.at[pl.ds(0, queries - rows), :]
            pltpu.make_async_copy(part, part, sem).wait()

        @pl.when(jnp.logical_not(short))
        def _():
            pltpu.make_async_copy(buffer, buffer, sem).wait()

    drain(q_all, q_send, own_row)
    drain(g_all, g_send, own_row)
    drain(dq_all, dq_send, mid_self)
    for copy in gaps + sides + [k_pass, v_pass] + returns:
        copy.wait_send()
    for head_z in range(4):

        @pl.when(head_z != col)
        def _(head_z=head_z):
            fin_copy(head_z, place_of(head_z)).wait_send()


def place_kernel(dq, dk, dv, db, dq_out, dk_out, dv_out, db_out, sems):
    copies = [
        pltpu.make_async_copy(src, dst, sems.at[n])
        for n, (src, dst) in enumerate(((dq, dq_out), (dk, dk_out), (dv, dv_out), (db, db_out)))
    ]
    for copy in copies:
        copy.start()
    for copy in copies:
        copy.wait()


def per_device(queries_in, key_states, value_states, grad_output, bias_table, gap_bucket, order):
    vmem = pl.BlockSpec(memory_space=pltpu.VMEM)
    anywhere = pl.BlockSpec(memory_space=pl.ANY)
    low, full = jnp.bfloat16, jnp.float32
    dma = pltpu.SemaphoreType.DMA
    outs = (
        jax.ShapeDtypeStruct((rows, 4 * dim), full),
        jax.ShapeDtypeStruct((keys, dim), full),
        jax.ShapeDtypeStruct((keys, dim), full),
        jax.ShapeDtypeStruct((1, levels), full),
    )
    results = pl.pallas_call(
        kernel,
        out_shape=outs,
        in_specs=[
            anywhere,
            anywhere,
            anywhere,
            anywhere,
            vmem,
            vmem,
            pl.BlockSpec(memory_space=pltpu.SMEM),
        ],
        out_specs=(vmem, vmem, vmem, vmem),
        scratch_shapes=[
            pltpu.VMEM((queries, dim), low),
            pltpu.VMEM((queries, dim), low),
            pltpu.VMEM((blocks, keys, dim), low),
            pltpu.VMEM((blocks, keys, dim), low),
            pltpu.VMEM((tiles, dim, tile), low),
            pltpu.VMEM((blocks, 8, 640), full),
            pltpu.VMEM((all_keys, dim), full),
            pltpu.VMEM((all_keys, dim), full),
            pltpu.VMEM((all_keys, dim), jnp.int32),
            pltpu.VMEM((1, queries), jnp.int32),
            pltpu.VMEM((all_keys, queries), full),
            pltpu.VMEM((all_keys, queries), full),
            pltpu.VMEM((blocks, 8, queries), full),
            pltpu.VMEM((8, queries), full),
            pltpu.VMEM((8, queries), full),
            pltpu.VMEM((dim, chunk), full),
            pltpu.VMEM((queries, dim), low),
            pltpu.VMEM((4, 2 * rows, dim), low),
            pltpu.VMEM((4, rows, dim), low),
            pltpu.VMEM((4, rows, dim), low),
            pltpu.VMEM((all_keys, dim), full),
            pltpu.VMEM((all_keys, dim), full),
            pltpu.VMEM((all_keys, dim), full),
            pltpu.VMEM((6, keys, dim), low),
            pltpu.VMEM((6, keys, dim), low),
            pltpu.VMEM((8, dim), full),
            pltpu.VMEM((7, 8, dim), full),
            dma((2,)),
            dma((3,)),
            dma((3,)),
            dma((3,)),
            dma((3,)),
            dma((3,)),
            dma((3,)),
            dma(()),
            dma((4,)),
            dma(()),
            dma((4,)),
            dma((chunks,)),
            dma((chunks,)),
            dma(()),
            dma((4,)),
            dma((4,)),
            dma(()),
            dma((6,)),
            dma((6,)),
            dma((7,)),
            dma((7,)),
        ],
        compiler_params=pltpu.CompilerParams(
            collective_id=0, has_side_effects=True, vmem_limit_bytes=60 * 1024 * 1024
        ),
        cost_estimate=pl.CostEstimate(
            flops=10 * all_keys * queries * dim,
            bytes_accessed=8 * queries * dim,
            transcendentals=2 * all_keys * queries,
        ),
    )(
        queries_in,
        grad_output,
        key_states,
        value_states,
        bias_table,
        gap_bucket,
        order,
    )
    return pl.pallas_call(
        place_kernel,
        out_shape=outs,
        in_specs=[anywhere] * 4,
        out_specs=(anywhere,) * 4,
        scratch_shapes=[dma((4,))],
    )(*results)


def solution(mesh):
    placed = (
        P("row", None),
        P(("col", "depth"), "row"),
        P(("col", "depth"), "row"),
        P("row", None),
        P(),
        P(("col", "depth")),
        P(),
    )
    return jax.shard_map(
        per_device,
        mesh=mesh,
        in_specs=placed,
        out_specs=(
            P("row", ("col", "depth")),
            P(("col", "depth"), "row"),
            P(("col", "depth"), "row"),
            P("row", None),
        ),
        check_vma=False,
    )
```

time: 74.7 us -> 88.7 us (1.19)
  Pallas kernels: 64.7 us -> 87.9 us
  local copies, waits for them, and re-layouts: 9.07 us -> 0 us
    pallas_call x1 -> x2, Pallas kernels: 64.7 us -> 87.9 us  [the longest x1 59.9 us: per_device(): pl.pallas_call(kernel, out_shape=outs, in_specs=[anywhere, anywhere, anyw...]
    unnamed x16 -> x0, local copies, waits for them, and re-layouts: 8.38 us -> none
where the time goes in v2:
time: 88.7 us; the launch traced here: 88.5 us
  Pallas kernels  87.9 us (99%)
    pallas_call x1, Pallas kernels, per_device(): pl.pallas_call(kernel, out_shape=outs, in_specs=[anywhere, anywhere, anyw...  59.9 us
    pallas_call x1, Pallas kernels, per_device(): pl.pallas_call(place_kernel, out_shape=outs, in_specs=[anywhere] * 4, out...  28 us

profile of v2, /device:TPU:71, one launch (start us, length us, event | category | flops | bytes accessed | tf_op | source)
XLA Modules:
  0.0 88.5 jit_solution(11810092117824680379)
XLA Ops:
  0.6 59.9 %shard_map.102 = (f32[144,512]{1,0:T(8,128)}, f32[576,128]{1,0:T(8,128)}, f32[576,128]{1,0:T(8,128)}, f32[1,64]{1,0:T(1,128)}) custom-call(bf16[144,4096]{1,0:T(8,128)(2,1)} %q_ref.1, bf16[144,4096]{1,0:T(8,128)(2,1)} %g_ref.1, bf16[576,128]{1,0:T(8,128)(2,1)} %k_ref.1, bf16[576,128]{1,0:T(8,128)(2,1)} %v_ref.1, f32[32,64]{1,0:T(8,128)} %table_ref.1, ...), custom_call_target="tpu_custom_call" | custom-call | flops 3397386240 | bytes 1179648 | tf_op jit(solution)/shard_map/pallas_call | solution.py:554
  60.5 28.0 %shard_map.103 = (f32[144,512]{1,0:T(8,128)}, f32[576,128]{1,0:T(8,128)}, f32[576,128]{1,0:T(8,128)}, f32[1,64]{1,0:T(1,128)}) custom-call(f32[144,512]{1,0:T(8,128)} %get-tuple-element.8.dq, f32[576,128]{1,0:T(8,128)} %get-tuple-element.9.dk, f32[576,128]{1,0:T(8,128)} %get-tuple-element.10.dv, f32[1,64]{1,0:T(1,128)} %get-tuple-element.11.db), custom_call_target="tpu_custom_call" | custom-call | tf_op jit(solution)/shard_map/pallas_call | solution.py:634

commit v3 on v2

--- a/solution.py
+++ b/solution.py
@@ -16,12 +16,9 @@
 levels = 64
 slots = 8
 queries = slots * rows
-chunk = 384
-chunks = queries // chunk
+cuts = (0, 512, 1152)
+chunks = len(cuts) - 1
 z_steps = (0, 1, 3, 2)
-tile = 288
-per_block = keys // tile
-tiles = blocks * per_block
 scale = dim ** -0.5
 log2e = math.log2(math.e)
 masked_value = -1e30
@@ -33,8 +30,8 @@
     return combine(a.reshape(a.shape[0] // 8, 8, a.shape[1]), axis=0)
 
 
-def wide(a):
-    return jnp.concatenate([a] * (chunk // dim), axis=1)
+def wide(a, count):
+    return jnp.concatenate([a] * (count // dim), axis=1)
 
 
 def nt_dot(a, b):
@@ -89,14 +86,11 @@
     query_pos,
     s_all,
     dp_all,
-    part_stats,
+    state,
     stats,
     stats_got,
-    dq_turned,
     dq_all,
-    mid_got,
-    mid_low,
-    fin_got,
+    dq_got,
     dk_sum,
     dv_sum,
     ds_sum,
@@ -119,8 +113,6 @@
     st_recv,
     dq_send,
     dq_recv,
-    fin_send,
-    fin_recv,
     dkv_send,
     dkv_recv,
     db_send,
@@ -137,7 +129,7 @@
     parity = col % 2
     other = (core + member) % 2
     own_row = col == 0
-    mid_self = (col == 0) & (depth == x // 2)
+    mid_self = (col == 0) & (z_lo == 0) & (depth == x // 2)
 
     def shift(j):
         return (parity + (1 if j in (1, 2) else 0)) % 2
@@ -171,12 +163,13 @@
     for n in range(1, 8):
         greet(peer(n // 2, n % 2))
     for n in range(8):
-        head_z, head_depth = n // 2, n % 2
-        head_x = depth * 2 + (x + z_lo + 4 - head_z + parity) % 2
-
-        @pl.when(jnp.logical_not(mid_self & (z_lo == head_z) & (depth == head_depth)))
-        def _(head_z=head_z, head_depth=head_depth, head_x=head_x):
-            greet((head_z * 8 + head_x * 2 + other, col, head_depth))
+        from_col, from_depth = n // 2, n % 2
+        head_x = depth * 2 + (x + z_lo + 4 - col + from_col) % 2
+        head_core = (core + from_col // 2) % 2
+
+        @pl.when(jnp.logical_not(mid_self & (from_col == 0) & (depth == from_depth)))
+        def _(device=(col * 8 + head_x * 2 + head_core, from_col, from_depth)):
+            greet(device)
 
     own_k = pltpu.make_async_copy(k_ref, k_all.at[0], local_sem.at[0])
     own_v = pltpu.make_async_copy(v_ref, v_all.at[0], local_sem.at[1])
@@ -275,14 +268,13 @@
         bias_cols[start : start + keys, :] = jnp.broadcast_to(bias * log2e, (keys, dim))
 
     def turn(b):
-        for t in range(per_block):
-            part = k_all[b, t * tile : (t + 1) * tile, :].astype(jnp.float32)
-            k_turned[b * per_block + t] = part.T.astype(jnp.bfloat16)
+        k_turned[b] = k_all[b].astype(jnp.float32).T.astype(jnp.bfloat16)
 
     fill_bias(0)
-    dk_sum[...] = jnp.zeros_like(dk_sum)
-    dv_sum[...] = jnp.zeros_like(dv_sum)
-    ds_sum[...] = jnp.zeros_like(ds_sum)
+    fresh = jnp.zeros((8, queries), jnp.float32)
+    state[0] = fresh + floor_value
+    state[1] = fresh
+    state[2] = fresh
     own_k.wait()
     own_v.wait()
     turn(0)
@@ -297,42 +289,38 @@
         pltpu.make_async_copy(part, part, sem.at[j]).wait()
 
     def first_pass(c, b):
-        lo, hi = c * chunk, (c + 1) * chunk
-        pos = query_pos[:, lo:hi]
-        q_part = q_all[lo:hi, :]
-        g_part = g_all[lo:hi, :]
-
-        def scores(t, best):
-            start = pl.multiple_of(t * tile, tile)
-            part = pl.ds(pl.multiple_of(b * keys + start, tile), tile)
-            s = nt_dot(k_all[b, pl.ds(start, tile), :], q_part) * (scale * log2e)
-            s = s + wide(bias_cols[part, :])
-            s = jnp.where(wide(key_pos[part, :]) <= pos, s, masked_value)
-            s_all[part, lo:hi] = s
-            return jnp.maximum(best, fold(s, jnp.max))
-
-        best = lax.fori_loop(0, per_block, scores, jnp.full((8, chunk), masked_value, jnp.float32))
-        best = jnp.maximum(jnp.max(best, axis=0, keepdims=True), floor_value)
-
-        def sums(t, state):
-            start = pl.multiple_of(t * tile, tile)
-            part = pl.ds(pl.multiple_of(b * keys + start, tile), tile)
-            dp = nt_dot(v_all[b, pl.ds(start, tile), :], g_part)
-            dp_all[part, lo:hi] = dp
-            w = jnp.exp2(s_all[part, lo:hi] - best)
-            return state[0] + fold(w, jnp.sum), state[1] + fold(w * dp, jnp.sum)
-
-        zero = jnp.zeros((8, chunk), jnp.float32)
-        total, moment = lax.fori_loop(0, per_block, sums, (zero, zero))
-        part_stats[b, 0:1, lo:hi] = best
-        part_stats[b, 1:2, lo:hi] = jnp.sum(total, axis=0, keepdims=True)
-        part_stats[b, 2:3, lo:hi] = jnp.sum(moment, axis=0, keepdims=True)
+        lo, hi = cuts[c], cuts[c + 1]
+        count = hi - lo
+        part = slice(b * keys, (b + 1) * keys)
+        s = nt_dot(k_all[b], q_all[lo:hi, :]) * (scale * log2e)
+        s = s + wide(bias_cols[part, :], count)
+        s = jnp.where(wide(key_pos[part, :], count) <= query_pos[:, lo:hi], s, masked_value)
+        s_all[part, lo:hi] = s
+        dp = nt_dot(v_all[b], g_all[lo:hi, :])
+        dp_all[part, lo:hi] = dp
+        before = state[0, :, lo:hi]
+        best = jnp.maximum(before, fold(s, jnp.max))
+        factor = jnp.exp2(before - best)
+        w = jnp.exp2(s.reshape(keys // 8, 8, count) - best[None])
+        wd = w * dp.reshape(keys // 8, 8, count)
+        state[0, :, lo:hi] = best
+        state[1, :, lo:hi] = state[1, :, lo:hi] * factor + jnp.sum(w, axis=0)
+        state[2, :, lo:hi] = state[2, :, lo:hi] * factor + jnp.sum(wd, axis=0)
 
     def stat_copy(c):
-        part = pl.ds(c * chunk, chunk)
+        part = pl.ds(cuts[c], cuts[c + 1] - cuts[c])
         return remote(
             stats.at[:, part], stats_got.at[:, part], st_send.at[c], st_recv.at[c], peer(0, 1)
         )
+
+    def close(c):
+        lo, hi = cuts[c], cuts[c + 1]
+        best = jnp.max(state[0, :, lo:hi], axis=0, keepdims=True)
+        factor = jnp.exp2(state[0, :, lo:hi] - best)
+        stats[0:1, lo:hi] = best
+        stats[1:2, lo:hi] = jnp.sum(state[1, :, lo:hi] * factor, axis=0, keepdims=True)
+        stats[2:3, lo:hi] = jnp.sum(state[2, :, lo:hi] * factor, axis=0, keepdims=True)
+        stat_copy(c).start()
 
     wait_group(q_all, q_recv, 0)
     wait_group(g_all, g_recv, 0)
@@ -349,26 +337,17 @@
     turn(3)
     first_pass(0, 1)
     first_pass(0, 3)
-    for c in range(1, chunks):
-        wait_group(q_all, q_recv, c + 1)
-        wait_group(g_all, g_recv, c + 1)
-
-        def near(i, carry, c=c):
-            first_pass(c, i + i // 2)
-            return carry
-
-        lax.fori_loop(0, 3, near, 0)
+    for j in (2, 3):
+        wait_group(q_all, q_recv, j)
+        wait_group(g_all, g_recv, j)
+    for b in (0, 1, 3):
+        first_pass(1, b)
     k_pass.wait_recv()
     v_pass.wait_recv()
+    for c in range(chunks):
+        first_pass(c, 2)
+        close(c)
     turn(2)
-    for c in range(chunks):
-        lo, hi = c * chunk, (c + 1) * chunk
-        first_pass(c, 2)
-        best, total, moment = merge([part_stats[b, 0:3, lo:hi] for b in range(blocks)])
-        stats[0:1, lo:hi] = best
-        stats[1:2, lo:hi] = total
-        stats[2:3, lo:hi] = moment
-        stat_copy(c).start()
 
     def kv_copy(n, a):
         return remote(
@@ -382,54 +361,55 @@
 
     sent = 0
     for c in range(chunks):
-        lo, hi = c * chunk, (c + 1) * chunk
+        lo, hi = cuts[c], cuts[c + 1]
         stat_copy(c).wait()
         best, total, moment = merge([stats[0:3, lo:hi], stats_got[0:3, lo:hi]])
         lse = best + jnp.log(total) * log2e
         delta = moment / total
-        q_part = q_all[lo:hi, :]
-        g_part = g_all[lo:hi, :]
-        dq_turned[...] = jnp.zeros_like(dq_turned)
-
-        def grads(t, carry):
-            start = pl.multiple_of(t * tile, tile)
-            part = pl.ds(start, tile)
+
+        def grads(b):
+            part = slice(b * keys, (b + 1) * keys)
             p = jnp.exp2(s_all[part, lo:hi] - lse)
             ds = p * (dp_all[part, lo:hi] - delta)
-            ds_sum[part, :] += sum(ds[:, n * dim : (n + 1) * dim] for n in range(chunk // dim))
+            ds_lanes = sum(ds[:, n * dim : (n + 1) * dim] for n in range((hi - lo) // dim))
             ds_low = ds.astype(jnp.bfloat16)
-            dv_sum[part, :] += nn_dot(p.astype(jnp.bfloat16), g_part)
-            dk_sum[part, :] += nn_dot(ds_low, q_part)
-            dq_turned[...] += nn_dot(k_turned[t], ds_low)
-            return carry
-
-        if c < chunks - 1:
-            lax.fori_loop(0, tiles, grads, 0)
-        else:
-            lax.fori_loop(2 * per_block, 3 * per_block, grads, 0)
+            dv_part = nn_dot(p.astype(jnp.bfloat16), g_all[lo:hi, :])
+            dk_part = nn_dot(ds_low, q_all[lo:hi, :])
+            if c == 0:
+                ds_sum[part, :] = ds_lanes
+                dv_sum[part, :] = dv_part
+                dk_sum[part, :] = dk_part
+            else:
+                ds_sum[part, :] += ds_lanes
+                dv_sum[part, :] += dv_part
+                dk_sum[part, :] += dk_part
+            return nn_dot(k_turned[b], ds_low)
+
+        dq = grads(2) + grads(3)
+        if c == chunks - 1:
             kv_low[0] = low(dk_sum, 2, scale)
             returns[0].start()
             kv_low[1] = low(dv_sum, 2, 1.0)
             returns[1].start()
-            lax.fori_loop(3 * per_block, 4 * per_block, grads, 0)
             kv_low[2] = low(dk_sum, 3, scale)
             returns[2].start()
-            lax.fori_loop(per_block, 2 * per_block, grads, 0)
+        dq = dq + (grads(1) + grads(0))
+        if c == chunks - 1:
             kv_low[3] = low(dv_sum, 1, 1.0)
             returns[3].start()
-            lax.fori_loop(0, per_block, grads, 0)
-        dq_all[lo:hi, :] = (dq_turned[...].T * scale).astype(jnp.bfloat16)
+        dq_all[lo:hi, :] = (dq.T * scale).astype(jnp.bfloat16)
         while (sent + 1) * rows <= hi:
             j = sent // 2
             src = dq_all.at[pl.ds(sent * rows, rows), :]
-            dst = mid_got.at[z_lo, pl.ds(pl.multiple_of(depth * rows, rows), rows), :]
-            target = ((((z_lo + z_steps[j]) % 4) * 8 + slot_x(sent) * 2 + other), col, x // 2)
-            away = remote(src, dst, dq_send, dq_recv.at[z_lo], target)
+            place = (x % 2) * 2 + core
+            dst = dq_got.at[place, pl.ds(pl.multiple_of(depth * rows, rows), rows), :]
+            target = (((z_lo + z_steps[j]) % 4) * 8 + slot_x(sent) * 2 + other, z_lo, x // 2)
+            away = remote(src, dst, dq_send, dq_recv.at[place], target)
             if sent == 0:
 
                 @pl.when(mid_self)
-                def _(src=src, dst=dst):
-                    pltpu.make_async_copy(src, dst, dq_recv.at[z_lo]).start()
+                def _(src=src, dst=dst, place=place):
+                    pltpu.make_async_copy(src, dst, dq_recv.at[place]).start()
 
                 @pl.when(jnp.logical_not(mid_self))
                 def _(away=away):
@@ -461,34 +441,6 @@
     )
     returns[5].start()
 
-    def fin_copy(head_z, place):
-        return remote(
-            mid_low.at[head_z],
-            fin_got.at[place],
-            fin_send.at[head_z],
-            fin_recv,
-            (row, head_z, depth),
-        )
-
-    def place_of(head_z):
-        return ((x + z_lo + 4 - head_z + parity) % 2) * 2 + other
-
-    for head_z in range(4):
-        both = mid_got.at[head_z]
-        pltpu.make_async_copy(both, both, dq_recv.at[head_z]).wait()
-        total = both[0:rows, :].astype(jnp.float32) + both[rows : 2 * rows, :].astype(jnp.float32)
-        mid_low[head_z] = total.astype(jnp.bfloat16)
-
-        @pl.when(head_z != col)
-        def _(head_z=head_z):
-            fin_copy(head_z, place_of(head_z)).start()
-
-        @pl.when(head_z == col)
-        def _(head_z=head_z):
-            pltpu.make_async_copy(
-                mid_low.at[head_z], fin_got.at[place_of(head_z)], fin_recv
-            ).start()
-
     returns[2].wait_recv()
     returns[4].wait_recv()
     dk_out[...] = (
@@ -503,9 +455,12 @@
         copy.wait()
     db_out[...] = db_own[0:1, 0:levels] + sum(db_got[n, 0:1, 0:levels] for n in range(7))
 
-    pltpu.make_async_copy(fin_got, fin_got, fin_recv).wait()
     for head in range(4):
-        dq_out[:, head * dim : (head + 1) * dim] = fin_got[head].astype(jnp.float32)
+        both = dq_got.at[head]
+        pltpu.make_async_copy(both, both, dq_recv.at[head]).wait()
+        dq_out[:, head * dim : (head + 1) * dim] = both[0:rows, :].astype(jnp.float32) + both[
+            rows : 2 * rows, :
+        ].astype(jnp.float32)
 
     def drain(buffer, sem, short):
         @pl.when(short)
@@ -522,27 +477,18 @@
     drain(dq_all, dq_send, mid_self)
     for copy in gaps + sides + [k_pass, v_pass] + returns:
         copy.wait_send()
-    for head_z in range(4):
-
-        @pl.when(head_z != col)
-        def _(head_z=head_z):
-            fin_copy(head_z, place_of(head_z)).wait_send()
-
-
-def place_kernel(dq, dk, dv, db, dq_out, dk_out, dv_out, db_out, sems):
-    copies = [
-        pltpu.make_async_copy(src, dst, sems.at[n])
-        for n, (src, dst) in enumerate(((dq, dq_out), (dk, dk_out), (dv, dv_out), (db, db_out)))
-    ]
-    for copy in copies:
-        copy.start()
-    for copy in copies:
-        copy.wait()
+
+
+def place_kernel(dq, dk, dv, db, dq_out, dk_out, dv_out, db_out):
+    dq_out[...] = dq[...]
+    dk_out[...] = dk[...]
+    dv_out[...] = dv[...]
+    db_out[...] = db[...]
 
 
 def per_device(queries_in, key_states, value_states, grad_output, bias_table, gap_bucket, order):
     vmem = pl.BlockSpec(memory_space=pltpu.VMEM)
-    anywhere = pl.BlockSpec(memory_space=pl.ANY)
+    hbm = pl.BlockSpec(memory_space=pltpu.HBM)
     low, full = jnp.bfloat16, jnp.float32
     dma = pltpu.SemaphoreType.DMA
     outs = (
@@ -555,10 +501,10 @@
         kernel,
         out_shape=outs,
         in_specs=[
-            anywhere,
-            anywhere,
-            anywhere,
-            anywhere,
+            hbm,
+            hbm,
+            hbm,
+            hbm,
             vmem,
             vmem,
             pl.BlockSpec(memory_space=pltpu.SMEM),
@@ -569,7 +515,7 @@
             pltpu.VMEM((queries, dim), low),
             pltpu.VMEM((blocks, keys, dim), low),
             pltpu.VMEM((blocks, keys, dim), low),
-            pltpu.VMEM((tiles, dim, tile), low),
+            pltpu.VMEM((blocks, dim, keys), low),
             pltpu.VMEM((blocks, 8, 640), full),
             pltpu.VMEM((all_keys, dim), full),
             pltpu.VMEM((all_keys, dim), full),
@@ -577,14 +523,11 @@
             pltpu.VMEM((1, queries), jnp.int32),
             pltpu.VMEM((all_keys, queries), full),
             pltpu.VMEM((all_keys, queries), full),
-            pltpu.VMEM((blocks, 8, queries), full),
+            pltpu.VMEM((3, 8, queries), full),
             pltpu.VMEM((8, queries), full),
             pltpu.VMEM((8, queries), full),
-            pltpu.VMEM((dim, chunk), full),
             pltpu.VMEM((queries, dim), low),
             pltpu.VMEM((4, 2 * rows, dim), low),
-            pltpu.VMEM((4, rows, dim), low),
-            pltpu.VMEM((4, rows, dim), low),
             pltpu.VMEM((all_keys, dim), full),
             pltpu.VMEM((all_keys, dim), full),
             pltpu.VMEM((all_keys, dim), full),
@@ -607,8 +550,6 @@
             dma((chunks,)),
             dma(()),
             dma((4,)),
-            dma((4,)),
-            dma(()),
             dma((6,)),
             dma((6,)),
             dma((7,)),
@@ -634,9 +575,8 @@
     return pl.pallas_call(
         place_kernel,
         out_shape=outs,
-        in_specs=[anywhere] * 4,
-        out_specs=(anywhere,) * 4,
-        scratch_shapes=[dma((4,))],
+        in_specs=[vmem] * 4,
+        out_specs=(vmem,) * 4,
     )(*results)
 
 

time: 88.7 us -> 53.3 us (0.60)
  Pallas kernels: 87.9 us -> 52.5 us
    pallas_call x2, Pallas kernels: 87.9 us -> 52.5 us  [the longest x1 50.4 us: per_device(): pl.pallas_call(kernel, out_shape=outs, in_specs=[hbm, hbm, hbm, hbm, vmem...]
where the time goes in v3:
time: 53.3 us; the launch traced here: 53.1 us
  Pallas kernels  52.5 us (98%)
  between operations  0.64 us (1%)
    pallas_call x1, Pallas kernels, per_device(): pl.pallas_call(kernel, out_shape=outs, in_specs=[hbm, hbm, hbm, hbm, vmem...  50.4 us
    pallas_call x1, Pallas kernels, per_device(): pl.pallas_call(place_kernel, out_shape=outs, in_specs=[vmem] * 4, out_spe...  2.07 us

profile of v3, /device:TPU:71, one launch (start us, length us, event | category | flops | bytes accessed | tf_op | source)
XLA Modules:
  0.0 53.1 jit_solution(5267146867963868555)
XLA Ops:
  0.6 50.4 %shard_map.102 = (f32[144,512]{1,0:T(8,128)}, f32[576,128]{1,0:T(8,128)}, f32[576,128]{1,0:T(8,128)}, f32[1,64]{1,0:T(1,128)}) custom-call(bf16[144,4096]{1,0:T(8,128)(2,1)} %q_ref.1, bf16[144,4096]{1,0:T(8,128)(2,1)} %g_ref.1, bf16[576,128]{1,0:T(8,128)(2,1)} %k_ref.1, bf16[576,128]{1,0:T(8,128)(2,1)} %v_ref.1, f32[32,64]{1,0:T(8,128)} %table_ref.1, ...), custom_call_target="tpu_custom_call" | custom-call | flops 3397386240 | bytes 1179648 | tf_op jit(solution)/shard_map/pallas_call | solution.py:500
  51.0 2.1 %shard_map.103 = (f32[144,512]{1,0:T(8,128)}, f32[576,128]{1,0:T(8,128)}, f32[576,128]{1,0:T(8,128)}, f32[1,64]{1,0:T(1,128)}) custom-call(f32[144,512]{1,0:T(8,128)} %get-tuple-element.8.dq, f32[576,128]{1,0:T(8,128)} %get-tuple-element.9.dk, f32[576,128]{1,0:T(8,128)} %get-tuple-element.10.dv, f32[1,64]{1,0:T(1,128)} %get-tuple-element.11.db), custom_call_target="tpu_custom_call" | custom-call | tf_op jit(solution)/shard_map/pallas_call | solution.py:575

commit v4 on v3

--- a/solution.py
+++ b/solution.py
@@ -11,6 +11,7 @@
 rows = 144
 dim = 128
 keys = 576
+half_keys = keys // 2
 blocks = 4
 all_keys = blocks * keys
 levels = 64
@@ -67,13 +68,20 @@
     g_ref,
     k_ref,
     v_ref,
-    table_ref,
-    gap_ref,
-    order_ref,
+    table_hbm,
+    gap_hbm,
+    order_hbm,
+    dq_hbm,
+    dk_hbm,
+    dv_hbm,
+    db_hbm,
     dq_out,
     dk_out,
     dv_out,
     db_out,
+    table_ref,
+    gap_ref,
+    order_ref,
     q_all,
     g_all,
     k_all,
@@ -99,6 +107,7 @@
     db_own,
     db_got,
     local_sem,
+    store_sem,
     gap_send,
     gap_recv,
     k_send,
@@ -144,24 +153,26 @@
     def peer(a, b):
         return (row, (col + a) % 4, (depth + b) % 2)
 
+    loads = [
+        pltpu.make_async_copy(src, dst, local_sem.at[n])
+        for n, (src, dst) in enumerate(
+            (
+                (k_ref, k_all.at[0]),
+                (v_ref, v_all.at[0]),
+                (gap_hbm, gap_ref),
+                (table_hbm, table_ref),
+                (order_hbm, order_ref),
+            )
+        )
+    ]
+    for copy in loads:
+        copy.start()
+
     barrier = pltpu.get_barrier_semaphore()
 
     def greet(device):
         pl.semaphore_signal(barrier, inc=1, device_id=device, device_id_type=MESH)
 
-    for step, j in ((0, 0), (1, 1), (-1, 2), (2, 3), (-2, 3)):
-        for i in range(2):
-            device = at(step, (x + shift(j) + 2 * i) % 4)
-            if step == 0 and i == 0:
-
-                @pl.when(jnp.logical_not(own_row))
-                def _(device=device):
-                    greet(device)
-
-            else:
-                greet(device)
-    for n in range(1, 8):
-        greet(peer(n // 2, n % 2))
     for n in range(8):
         from_col, from_depth = n // 2, n % 2
         head_x = depth * 2 + (x + z_lo + 4 - col + from_col) % 2
@@ -171,15 +182,26 @@
         def _(device=(col * 8 + head_x * 2 + head_core, from_col, from_depth)):
             greet(device)
 
-    own_k = pltpu.make_async_copy(k_ref, k_all.at[0], local_sem.at[0])
-    own_v = pltpu.make_async_copy(v_ref, v_all.at[0], local_sem.at[1])
-    own_k.start()
-    own_v.start()
-    gap_rows[0] = jnp.zeros((8, 640), jnp.float32)
+    for n in (5, 7, 3, 4, 1, 6, 2):
+        greet(peer(n // 2, n % 2))
+    for step, j in ((2, 3), (-2, 3), (1, 1), (-1, 2), (0, 0)):
+        for i in range(2):
+            device = at(step, (x + shift(j) + 2 * i) % 4)
+            if step == 0 and i == 0:
+
+                @pl.when(jnp.logical_not(own_row))
+                def _(device=device):
+                    greet(device)
+
+            else:
+                greet(device)
+    loads[2].wait()
+    gap_rows[0] = jnp.zeros((1, 640), jnp.float32)
     gap_rows[0, 0:1, 0:keys] = gap_ref[...].astype(jnp.float32).reshape(1, keys)
 
     pl.semaphore_wait(
-        barrier, 25 - own_row.astype(jnp.int32) - mid_self.astype(jnp.int32)
+        barrier,
+        25 - own_row.astype(jnp.int32) - mid_self.astype(jnp.int32),
     )
 
     def remote(src, dst, send_sem, recv_sem, device):
@@ -197,19 +219,32 @@
             gap_rows.at[0], gap_rows.at[4 - a], gap_send.at[a - 1], gap_recv.at[3 - a], peer(a, 0)
         )
 
-    def own_copy(a, src, dst, send, recv):
-        return remote(src, dst.at[4 - a], send.at[a - 1], recv.at[3 - a], peer(a, 0))
-
-    def pass_copy(a, dst, send, recv):
-        return remote(dst.at[4 - a], dst.at[2], send.at[1], recv.at[1], peer(a, 0))
+    def own_copy(a, h, src, dst, send, recv):
+        part = pl.ds(h * half_keys, half_keys)
+        return remote(
+            src.at[part, :],
+            dst.at[4 - a, part, :],
+            send.at[a - 1, h],
+            recv.at[3 - a, h],
+            peer(a, 0),
+        )
+
+    def pass_copy(a, h, dst, send, recv):
+        part = pl.ds(h * half_keys, half_keys)
+        return remote(
+            dst.at[4 - a, part, :], dst.at[2, part, :], send.at[1, h], recv.at[1, h], peer(a, 0)
+        )
 
     gaps = [gap_copy(a) for a in (1, 3, 2)]
-    sides = [own_copy(a, k_ref, k_all, k_send, k_recv) for a in (1, 3)] + [
-        own_copy(a, v_ref, v_all, v_send, v_recv) for a in (3, 1)
-    ]
-    k_pass = pass_copy(1, k_all, k_send, k_recv)
-    v_pass = pass_copy(3, v_all, v_send, v_recv)
-    for copy in (sides[0], sides[2]):
+    passed, direct, onward = [], [], []
+    for h in range(2):
+        passed.append(own_copy(1, h, k_ref, k_all, k_send, k_recv))
+        passed.append(own_copy(3, h, v_ref, v_all, v_send, v_recv))
+        direct.append(own_copy(3, h, k_ref, k_all, k_send, k_recv))
+        direct.append(own_copy(1, h, v_ref, v_all, v_send, v_recv))
+        onward.append(pass_copy(1, h, k_all, k_send, k_recv))
+        onward.append(pass_copy(3, h, v_all, v_send, v_recv))
+    for copy in passed:
         copy.start()
 
     def send_rows(src, dst, send_sem, recv_sem, step, j):
@@ -241,8 +276,11 @@
     send_rows(g_ref, g_all, g_send, g_recv, -1, 1)
     send_rows(g_ref, g_all, g_send, g_recv, 1, 2)
     send_rows(g_ref, g_all, g_send, g_recv, 2, 3)
-    for copy in (sides[1], sides[3]):
+    for copy in direct:
         copy.start()
+
+    for n in (0, 1, 3, 4):
+        loads[n].wait()
 
     lane = lax.broadcasted_iota(jnp.int32, (1, queries), 1)
     half = rows // 2
@@ -275,14 +313,11 @@
     state[0] = fresh + floor_value
     state[1] = fresh
     state[2] = fresh
-    own_k.wait()
-    own_v.wait()
     turn(0)
 
-    sides[0].wait_recv()
-    k_pass.start()
-    sides[2].wait_recv()
-    v_pass.start()
+    for come, go in zip(passed, onward):
+        come.wait_recv()
+        go.start()
 
     def wait_group(buffer, sem, j):
         part = buffer.at[pl.ds(j * 2 * rows, 2 * rows), :]
@@ -331,8 +366,8 @@
         copy.wait_recv()
     for b in (3, 1, 2):
         fill_bias(b)
-    sides[1].wait_recv()
-    sides[3].wait_recv()
+    for copy in direct:
+        copy.wait_recv()
     turn(1)
     turn(3)
     first_pass(0, 1)
@@ -342,8 +377,8 @@
         wait_group(g_all, g_recv, j)
     for b in (0, 1, 3):
         first_pass(1, b)
-    k_pass.wait_recv()
-    v_pass.wait_recv()
+    for copy in onward:
+        copy.wait_recv()
     for c in range(chunks):
         first_pass(c, 2)
         close(c)
@@ -359,57 +394,49 @@
     def low(total, b, factor):
         return (total[b * keys : (b + 1) * keys, :] * factor).astype(jnp.bfloat16)
 
-    sent = 0
-    for c in range(chunks):
+    def dq_place(head_x, s):
+        place = (head_x % 2) * 2 + core
+        dst = dq_got.at[place, pl.ds(pl.multiple_of(depth * rows, rows), rows), :]
+        there = (head_x + shift(s // 2) + 2 * (s % 2)) % 4
+        target = (((z_lo + z_steps[s // 2]) % 4) * 8 + there * 2 + other, z_lo, head_x // 2)
+        return dst, dq_recv.at[place], target
+
+    def factors(c):
         lo, hi = cuts[c], cuts[c + 1]
         stat_copy(c).wait()
         best, total, moment = merge([stats[0:3, lo:hi], stats_got[0:3, lo:hi]])
-        lse = best + jnp.log(total) * log2e
-        delta = moment / total
-
-        def grads(b):
-            part = slice(b * keys, (b + 1) * keys)
-            p = jnp.exp2(s_all[part, lo:hi] - lse)
-            ds = p * (dp_all[part, lo:hi] - delta)
-            ds_lanes = sum(ds[:, n * dim : (n + 1) * dim] for n in range((hi - lo) // dim))
-            ds_low = ds.astype(jnp.bfloat16)
-            dv_part = nn_dot(p.astype(jnp.bfloat16), g_all[lo:hi, :])
-            dk_part = nn_dot(ds_low, q_all[lo:hi, :])
-            if c == 0:
-                ds_sum[part, :] = ds_lanes
-                dv_sum[part, :] = dv_part
-                dk_sum[part, :] = dk_part
-            else:
-                ds_sum[part, :] += ds_lanes
-                dv_sum[part, :] += dv_part
-                dk_sum[part, :] += dk_part
-            return nn_dot(k_turned[b], ds_low)
-
-        dq = grads(2) + grads(3)
-        if c == chunks - 1:
-            kv_low[0] = low(dk_sum, 2, scale)
-            returns[0].start()
-            kv_low[1] = low(dv_sum, 2, 1.0)
-            returns[1].start()
-            kv_low[2] = low(dk_sum, 3, scale)
-            returns[2].start()
-        dq = dq + (grads(1) + grads(0))
-        if c == chunks - 1:
-            kv_low[3] = low(dv_sum, 1, 1.0)
-            returns[3].start()
-        dq_all[lo:hi, :] = (dq.T * scale).astype(jnp.bfloat16)
-        while (sent + 1) * rows <= hi:
-            j = sent // 2
-            src = dq_all.at[pl.ds(sent * rows, rows), :]
-            place = (x % 2) * 2 + core
-            dst = dq_got.at[place, pl.ds(pl.multiple_of(depth * rows, rows), rows), :]
-            target = (((z_lo + z_steps[j]) % 4) * 8 + slot_x(sent) * 2 + other, z_lo, x // 2)
-            away = remote(src, dst, dq_send, dq_recv.at[place], target)
-            if sent == 0:
+        return best + jnp.log(total) * log2e, moment / total
+
+    def grads(c, b, lse, delta):
+        lo, hi = cuts[c], cuts[c + 1]
+        part = slice(b * keys, (b + 1) * keys)
+        p = jnp.exp2(s_all[part, lo:hi] - lse)
+        ds = p * (dp_all[part, lo:hi] - delta)
+        ds_lanes = sum(ds[:, n * dim : (n + 1) * dim] for n in range((hi - lo) // dim))
+        ds_low = ds.astype(jnp.bfloat16)
+        dv_part = nn_dot(p.astype(jnp.bfloat16), g_all[lo:hi, :])
+        dk_part = nn_dot(ds_low, q_all[lo:hi, :])
+        if c == 0:
+            ds_sum[part, :] = ds_lanes
+            dv_sum[part, :] = dv_part
+            dk_sum[part, :] = dk_part
+        else:
+            ds_sum[part, :] += ds_lanes
+            dv_sum[part, :] += dv_part
+            dk_sum[part, :] += dk_part
+        return nn_dot(k_turned[b], ds_low)
+
+    def send_dq(c, dq):
+        dq_all[cuts[c] : cuts[c + 1], :] = (dq.T * scale).astype(jnp.bfloat16)
+        for s in range(cuts[c] // rows, cuts[c + 1] // rows):
+            src = dq_all.at[pl.ds(s * rows, rows), :]
+            dst, recv, target = dq_place(x, s)
+            away = remote(src, dst, dq_send, recv, target)
+            if s == 0:
 
                 @pl.when(mid_self)
-                def _(src=src, dst=dst, place=place):
-                    pltpu.make_async_copy(src, dst, dq_recv.at[place]).start()
+                def _(src=src, dst=dst, recv=recv):
+                    pltpu.make_async_copy(src, dst, recv).start()
 
                 @pl.when(jnp.logical_not(mid_self))
                 def _(away=away):
@@ -417,7 +444,22 @@
 
             else:
                 away.start()
-            sent += 1
+
+    def send_kv(n, total, b, factor):
+        kv_low[n] = low(total, b, factor)
+        returns[n].start()
+
+    lse, delta = factors(0)
+    send_dq(0, sum(grads(0, b, lse, delta) for b in (2, 3, 1, 0)))
+    lse, delta = factors(1)
+    dq = grads(1, 2, lse, delta)
+    send_kv(0, dk_sum, 2, scale)
+    send_kv(1, dv_sum, 2, 1.0)
+    dq = dq + grads(1, 3, lse, delta)
+    send_kv(2, dk_sum, 3, scale)
+    dq = dq + grads(1, 1, lse, delta)
+    send_kv(3, dv_sum, 1, 1.0)
+    send_dq(1, dq + grads(1, 0, lse, delta))
 
     column = jnp.sum(ds_sum[...], axis=1, keepdims=True)
     by_level = jnp.where(gap_cols[:, 0:levels] == level, column, 0.0)
@@ -441,19 +483,26 @@
     )
     returns[5].start()
 
+    stores = [
+        pltpu.make_async_copy(src, dst, store_sem.at[n])
+        for n, (src, dst) in enumerate(((dk_out, dk_hbm), (dv_out, dv_hbm), (db_out, db_hbm)))
+    ]
     returns[2].wait_recv()
     returns[4].wait_recv()
     dk_out[...] = (
         dk_sum[0:keys, :] * scale + kv_got[2].astype(jnp.float32) + kv_got[4].astype(jnp.float32)
     )
+    stores[0].start()
     returns[3].wait_recv()
     returns[5].wait_recv()
     dv_out[...] = (
         dv_sum[0:keys, :] + kv_got[3].astype(jnp.float32) + kv_got[5].astype(jnp.float32)
     )
+    stores[1].start()
     for copy in biases:
         copy.wait()
     db_out[...] = db_own[0:1, 0:levels] + sum(db_got[n, 0:1, 0:levels] for n in range(7))
+    stores[2].start()
 
     for head in range(4):
         both = dq_got.at[head]
@@ -461,6 +510,11 @@
         dq_out[:, head * dim : (head + 1) * dim] = both[0:rows, :].astype(jnp.float32) + both[
             rows : 2 * rows, :
         ].astype(jnp.float32)
+        part = pl.ds(head * dim, dim)
+        stores.append(
+            pltpu.make_async_copy(dq_out.at[:, part], dq_hbm.at[:, part], store_sem.at[3 + head])
+        )
+        stores[3 + head].start()
 
     def drain(buffer, sem, short):
         @pl.when(short)
@@ -475,7 +529,10 @@
     drain(q_all, q_send, own_row)
     drain(g_all, g_send, own_row)
     drain(dq_all, dq_send, mid_self)
-    for copy in gaps + sides + [k_pass, v_pass] + returns:
+
+    for copy in stores:
+        copy.wait()
+    for copy in gaps + passed + direct + onward + returns:
         copy.wait_send()
 
 
@@ -505,18 +562,22 @@
             hbm,
             hbm,
             hbm,
-            vmem,
-            vmem,
-            pl.BlockSpec(memory_space=pltpu.SMEM),
+            hbm,
+            hbm,
+            hbm,
         ],
-        out_specs=(vmem, vmem, vmem, vmem),
-        scratch_shapes=[
+        out_specs=(hbm, hbm, hbm, hbm),
+        scratch_shapes=[pltpu.VMEM(a.shape, full) for a in outs]
+        + [
+            pltpu.VMEM((32, levels), full),
+            pltpu.VMEM((keys,), jnp.int32),
+            pltpu.SMEM((64,), jnp.int32),
             pltpu.VMEM((queries, dim), low),
             pltpu.VMEM((queries, dim), low),
             pltpu.VMEM((blocks, keys, dim), low),
             pltpu.VMEM((blocks, keys, dim), low),
             pltpu.VMEM((blocks, dim, keys), low),
-            pltpu.VMEM((blocks, 8, 640), full),
+            pltpu.VMEM((blocks, 1, 640), full),
             pltpu.VMEM((all_keys, dim), full),
             pltpu.VMEM((all_keys, dim), full),
             pltpu.VMEM((all_keys, dim), jnp.int32),
@@ -535,13 +596,14 @@
             pltpu.VMEM((6, keys, dim), low),
             pltpu.VMEM((8, dim), full),
             pltpu.VMEM((7, 8, dim), full),
-            dma((2,)),
+            dma((5,)),
+            dma((7,)),
             dma((3,)),
             dma((3,)),
-            dma((3,)),
-            dma((3,)),
-            dma((3,)),
-            dma((3,)),
+            dma((3, 2)),
+            dma((3, 2)),
+            dma((3, 2)),
+            dma((3, 2)),
             dma(()),
             dma((4,)),
             dma(()),

time: 53.3 us -> 52.4 us (0.983)
  Pallas kernels: 52.5 us -> 51.6 us
    pallas_call x1, Pallas kernels: 50.4 us -> 49.6 us  [per_device(): pl.pallas_call(kernel, out_shape=outs, in_specs=[hbm, hbm, hbm, hbm, hbm,...]
where the time goes in v4:
time: 52.4 us; the launch traced here: 52.3 us
  Pallas kernels  51.6 us (98%)
  between operations  0.64 us (1%)
    pallas_call x1, Pallas kernels, per_device(): pl.pallas_call(kernel, out_shape=outs, in_specs=[hbm, hbm, hbm, hbm, hbm,...  49.6 us
    pallas_call x1, Pallas kernels, per_device(): pl.pallas_call(place_kernel, out_shape=outs, in_specs=[vmem] * 4, out_spe...  2.07 us

profile of v4, /device:TPU:71, one launch (start us, length us, event | category | flops | bytes accessed | tf_op | source)
XLA Modules:
  0.0 52.3 jit_solution(5502427709615226312)
XLA Ops:
  0.6 49.6 %shard_map.102 = (f32[144,512]{1,0:T(8,128)}, f32[576,128]{1,0:T(8,128)}, f32[576,128]{1,0:T(8,128)}, f32[1,64]{1,0:T(1,128)}) custom-call(bf16[144,4096]{1,0:T(8,128)(2,1)} %q_ref.1, bf16[144,4096]{1,0:T(8,128)(2,1)} %g_ref.1, bf16[576,128]{1,0:T(8,128)(2,1)} %k_ref.1, bf16[576,128]{1,0:T(8,128)(2,1)} %v_ref.1, f32[32,64]{1,0:T(8,128)} %table_hbm.1, ...), custom_call_target="tpu_custom_call" | custom-call | flops 3397386240 | bytes 1179648 | tf_op jit(solution)/shard_map/pallas_call | solution.py:557
  50.2 2.1 %shard_map.103 = (f32[144,512]{1,0:T(8,128)}, f32[576,128]{1,0:T(8,128)}, f32[576,128]{1,0:T(8,128)}, f32[1,64]{1,0:T(1,128)}) custom-call(f32[144,512]{1,0:T(8,128)} %get-tuple-element.8.dq, f32[576,128]{1,0:T(8,128)} %get-tuple-element.9.dk, f32[576,128]{1,0:T(8,128)} %get-tuple-element.10.dv, f32[1,64]{1,0:T(1,128)} %get-tuple-element.11.db), custom_call_target="tpu_custom_call" | custom-call | tf_op jit(solution)/shard_map/pallas_call | solution.py:637

commit v5 on v4

--- a/solution.py
+++ b/solution.py
@@ -99,6 +99,7 @@
     stats_got,
     dq_all,
     dq_got,
+    held,
     dk_sum,
     dv_sum,
     ds_sum,
@@ -122,6 +123,8 @@
     st_recv,
     dq_send,
     dq_recv,
+    held_recv,
+    on_send,
     dkv_send,
     dkv_recv,
     db_send,
@@ -138,7 +141,7 @@
     parity = col % 2
     other = (core + member) % 2
     own_row = col == 0
-    mid_self = (col == 0) & (z_lo == 0) & (depth == x // 2)
+    dq_self = (member == 0) & (col == z_lo)
 
     def shift(j):
         return (parity + (1 if j in (1, 2) else 0)) % 2
@@ -149,6 +152,9 @@
 
     def slot_x(s):
         return (x + shift(s // 2) + 2 * (s % 2)) % 4
+
+    def beside(d):
+        return (z_lo * 8 + ((x + d) % 4) * 2 + core, col, depth)
 
     def peer(a, b):
         return (row, (col + a) % 4, (depth + b) % 2)
@@ -175,15 +181,16 @@
 
     for n in range(8):
         from_col, from_depth = n // 2, n % 2
-        head_x = depth * 2 + (x + z_lo + 4 - col + from_col) % 2
         head_core = (core + from_col // 2) % 2
 
-        @pl.when(jnp.logical_not(mid_self & (from_col == 0) & (depth == from_depth)))
-        def _(device=(col * 8 + head_x * 2 + head_core, from_col, from_depth)):
+        @pl.when(jnp.logical_not(dq_self & (from_col == col) & (depth == from_depth)))
+        def _(device=(col * 8 + x * 2 + head_core, from_col, from_depth)):
             greet(device)
 
     for n in (5, 7, 3, 4, 1, 6, 2):
         greet(peer(n // 2, n % 2))
+    for d in (2, 1, 3):
+        greet(beside(d))
     for step, j in ((2, 3), (-2, 3), (1, 1), (-1, 2), (0, 0)):
         for i in range(2):
             device = at(step, (x + shift(j) + 2 * i) % 4)
@@ -201,7 +208,7 @@
 
     pl.semaphore_wait(
         barrier,
-        25 - own_row.astype(jnp.int32) - mid_self.astype(jnp.int32),
+        28 - own_row.astype(jnp.int32) - dq_self.astype(jnp.int32),
     )
 
     def remote(src, dst, send_sem, recv_sem, device):
@@ -394,12 +401,40 @@
     def low(total, b, factor):
         return (total[b * keys : (b + 1) * keys, :] * factor).astype(jnp.bfloat16)
 
-    def dq_place(head_x, s):
+    def slot_d(s):
+        return (shift(s // 2) + 2 * (s % 2)) % 4
+
+    def onto(s, src):
+        head_x = (x + 4 - slot_d(s)) % 4
         place = (head_x % 2) * 2 + core
         dst = dq_got.at[place, pl.ds(pl.multiple_of(depth * rows, rows), rows), :]
-        there = (head_x + shift(s // 2) + 2 * (s % 2)) % 4
-        target = (((z_lo + z_steps[s // 2]) % 4) * 8 + there * 2 + other, z_lo, head_x // 2)
-        return dst, dq_recv.at[place], target
+        target = (((z_lo + z_steps[s // 2]) % 4) * 8 + x * 2 + other, z_lo, head_x // 2)
+        mine = dq_self & (head_x // 2 == depth) if s // 2 == 0 else None
+        return remote(src, dst, on_send.at[s], dq_recv.at[place], target), mine, place, dst
+
+    def send_on(s, src):
+        away, mine, place, dst = onto(s, src)
+        if mine is None:
+            away.start()
+        else:
+
+            @pl.when(mine)
+            def _():
+                pltpu.make_async_copy(src, dst, dq_recv.at[place]).start()
+
+            @pl.when(jnp.logical_not(mine))
+            def _():
+                away.start()
+
+    def hand_on(s):
+        def go():
+            pltpu.make_async_copy(held.at[s], held.at[s], held_recv.at[s]).wait()
+            send_on(s, held.at[s])
+
+        if s % 2:
+            go()
+        else:
+            pl.when(shift(s // 2) == 1)(go)
 
     def factors(c):
         lo, hi = cuts[c], cuts[c + 1]
@@ -430,20 +465,18 @@
         dq_all[cuts[c] : cuts[c + 1], :] = (dq.T * scale).astype(jnp.bfloat16)
         for s in range(cuts[c] // rows, cuts[c + 1] // rows):
             src = dq_all.at[pl.ds(s * rows, rows), :]
-            dst, recv, target = dq_place(x, s)
-            away = remote(src, dst, dq_send, recv, target)
-            if s == 0:
-
-                @pl.when(mid_self)
-                def _(src=src, dst=dst, recv=recv):
-                    pltpu.make_async_copy(src, dst, recv).start()
-
-                @pl.when(jnp.logical_not(mid_self))
-                def _(away=away):
-                    away.start()
-
+            aside = remote(src, held.at[s], dq_send, held_recv.at[s], beside(slot_d(s)))
+            if s % 2:
+                aside.start()
             else:
-                away.start()
+
+                @pl.when(shift(s // 2) == 0)
+                def _(s=s, src=src):
+                    send_on(s, src)
+
+                @pl.when(shift(s // 2) == 1)
+                def _(aside=aside):
+                    aside.start()
 
     def send_kv(n, total, b, factor):
         kv_low[n] = low(total, b, factor)
@@ -472,6 +505,8 @@
     for copy in biases:
         copy.start()
 
+    for s in range(3):
+        hand_on(s)
     returns[0].wait_recv()
     kv_low[4] = (dk_sum[keys : 2 * keys, :] * scale + kv_got[0].astype(jnp.float32)).astype(
         jnp.bfloat16
@@ -482,6 +517,8 @@
         jnp.bfloat16
     )
     returns[5].start()
+    for s in range(3, slots):
+        hand_on(s)
 
     stores = [
         pltpu.make_async_copy(src, dst, store_sem.at[n])
@@ -528,7 +565,14 @@
 
     drain(q_all, q_send, own_row)
     drain(g_all, g_send, own_row)
-    drain(dq_all, dq_send, mid_self)
+    part = dq_all.at[pl.ds(0, 6 * rows), :]
+    pltpu.make_async_copy(part, part, dq_send).wait()
+    for s in range(slots):
+        away, mine, _, _ = onto(s, held.at[s])
+        if mine is None:
+            away.wait_send()
+        else:
+            pl.when(jnp.logical_not(mine))(away.wait_send)
 
     for copy in stores:
         copy.wait()
@@ -589,6 +633,7 @@
             pltpu.VMEM((8, queries), full),
             pltpu.VMEM((queries, dim), low),
             pltpu.VMEM((4, 2 * rows, dim), low),
+            pltpu.VMEM((slots, rows, dim), low),
             pltpu.VMEM((all_keys, dim), full),
             pltpu.VMEM((all_keys, dim), full),
             pltpu.VMEM((all_keys, dim), full),
@@ -612,6 +657,8 @@
             dma((chunks,)),
             dma(()),
             dma((4,)),
+            dma((slots,)),
+            dma((slots,)),
             dma((6,)),
             dma((6,)),
             dma((7,)),

time: 52.4 us -> 50.7 us (0.968)
  the two profiles are of different devices: /device:TPU:71 before, /device:TPU:6 now
where the time goes in v5:
time: 50.7 us; the launch traced here: 50.6 us
  Pallas kernels  49.9 us (98%)
  between operations  0.64 us (1%)
    pallas_call x1, Pallas kernels, per_device(): pl.pallas_call(kernel, out_shape=outs, in_specs=[hbm, hbm, hbm, hbm, hbm,...  47.9 us
    pallas_call x1, Pallas kernels, per_device(): pl.pallas_call(place_kernel, out_shape=outs, in_specs=[vmem] * 4, out_spe...  2.07 us

profile of v5, /device:TPU:6, one launch (start us, length us, event | category | flops | bytes accessed | tf_op | source)
XLA Modules:
  0.0 50.6 jit_solution(6021224624281108424)
XLA Ops:
  0.6 47.9 %shard_map.102 = (f32[144,512]{1,0:T(8,128)}, f32[576,128]{1,0:T(8,128)}, f32[576,128]{1,0:T(8,128)}, f32[1,64]{1,0:T(1,128)}) custom-call(bf16[144,4096]{1,0:T(8,128)(2,1)} %q_ref.1, bf16[144,4096]{1,0:T(8,128)(2,1)} %g_ref.1, bf16[576,128]{1,0:T(8,128)(2,1)} %k_ref.1, bf16[576,128]{1,0:T(8,128)(2,1)} %v_ref.1, f32[32,64]{1,0:T(8,128)} %table_hbm.1, ...), custom_call_target="tpu_custom_call" | custom-call | flops 3397386240 | bytes 1179648 | tf_op jit(solution)/shard_map/pallas_call | solution.py:601
  48.5 2.1 %shard_map.103 = (f32[144,512]{1,0:T(8,128)}, f32[576,128]{1,0:T(8,128)}, f32[576,128]{1,0:T(8,128)}, f32[1,64]{1,0:T(1,128)}) custom-call(f32[144,512]{1,0:T(8,128)} %get-tuple-element.8.dq, f32[576,128]{1,0:T(8,128)} %get-tuple-element.9.dk, f32[576,128]{1,0:T(8,128)} %get-tuple-element.10.dv, f32[1,64]{1,0:T(1,128)} %get-tuple-element.11.db), custom_call_target="tpu_custom_call" | custom-call | tf_op jit(solution)/shard_map/pallas_call | solution.py:684

commit v6 on v5

--- a/solution.py
+++ b/solution.py
@@ -71,11 +71,10 @@
     table_hbm,
     gap_hbm,
     order_hbm,
-    dq_hbm,
+    dq_got,
     dk_hbm,
     dv_hbm,
     db_hbm,
-    dq_out,
     dk_out,
     dv_out,
     db_out,
@@ -98,7 +97,6 @@
     stats,
     stats_got,
     dq_all,
-    dq_got,
     held,
     dk_sum,
     dv_sum,
@@ -278,10 +276,10 @@
     for copy in gaps:
         copy.start()
     send_rows(q_ref, q_all, q_send, q_recv, -1, 1)
+    send_rows(g_ref, g_all, g_send, g_recv, -1, 1)
     send_rows(q_ref, q_all, q_send, q_recv, 1, 2)
+    send_rows(g_ref, g_all, g_send, g_recv, 1, 2)
     send_rows(q_ref, q_all, q_send, q_recv, -2, 3)
-    send_rows(g_ref, g_all, g_send, g_recv, -1, 1)
-    send_rows(g_ref, g_all, g_send, g_recv, 1, 2)
     send_rows(g_ref, g_all, g_send, g_recv, 2, 3)
     for copy in direct:
         copy.start()
@@ -325,6 +323,10 @@
     for come, go in zip(passed, onward):
         come.wait_recv()
         go.start()
+    for copy in gaps:
+        copy.wait_recv()
+    for b in (3, 1, 2):
+        fill_bias(b)
 
     def wait_group(buffer, sem, j):
         part = buffer.at[pl.ds(j * 2 * rows, 2 * rows), :]
@@ -369,14 +371,8 @@
     wait_group(q_all, q_recv, 1)
     wait_group(g_all, g_recv, 1)
     first_pass(0, 0)
-    for copy in gaps:
-        copy.wait_recv()
-    for b in (3, 1, 2):
-        fill_bias(b)
     for copy in direct:
         copy.wait_recv()
-    turn(1)
-    turn(3)
     first_pass(0, 1)
     first_pass(0, 3)
     for j in (2, 3):
@@ -389,7 +385,8 @@
     for c in range(chunks):
         first_pass(c, 2)
         close(c)
-    turn(2)
+    for b in (2, 3, 1):
+        turn(b)
 
     def kv_copy(n, a):
         return remote(
@@ -544,14 +541,6 @@
     for head in range(4):
         both = dq_got.at[head]
         pltpu.make_async_copy(both, both, dq_recv.at[head]).wait()
-        dq_out[:, head * dim : (head + 1) * dim] = both[0:rows, :].astype(jnp.float32) + both[
-            rows : 2 * rows, :
-        ].astype(jnp.float32)
-        part = pl.ds(head * dim, dim)
-        stores.append(
-            pltpu.make_async_copy(dq_out.at[:, part], dq_hbm.at[:, part], store_sem.at[3 + head])
-        )
-        stores[3 + head].start()
 
     def drain(buffer, sem, short):
         @pl.when(short)
@@ -581,7 +570,10 @@
 
 
 def place_kernel(dq, dk, dv, db, dq_out, dk_out, dv_out, db_out):
-    dq_out[...] = dq[...]
+    for head in range(4):
+        dq_out[:, head * dim : (head + 1) * dim] = dq[head, 0:rows, :].astype(
+            jnp.float32
+        ) + dq[head, rows : 2 * rows, :].astype(jnp.float32)
     dk_out[...] = dk[...]
     dv_out[...] = dv[...]
     db_out[...] = db[...]
@@ -600,7 +592,7 @@
     )
     results = pl.pallas_call(
         kernel,
-        out_shape=outs,
+        out_shape=(jax.ShapeDtypeStruct((4, 2 * rows, dim), low),) + outs[1:],
         in_specs=[
             hbm,
             hbm,
@@ -611,7 +603,7 @@
             hbm,
         ],
         out_specs=(hbm, hbm, hbm, hbm),
-        scratch_shapes=[pltpu.VMEM(a.shape, full) for a in outs]
+        scratch_shapes=[pltpu.VMEM(a.shape, full) for a in outs[1:]]
         + [
             pltpu.VMEM((32, levels), full),
             pltpu.VMEM((keys,), jnp.int32),
@@ -632,7 +624,6 @@
             pltpu.VMEM((8, queries), full),
             pltpu.VMEM((8, queries), full),
             pltpu.VMEM((queries, dim), low),
-            pltpu.VMEM((4, 2 * rows, dim), low),
             pltpu.VMEM((slots, rows, dim), low),
             pltpu.VMEM((all_keys, dim), full),
             pltpu.VMEM((all_keys, dim), full),
@@ -642,7 +633,7 @@
             pltpu.VMEM((8, dim), full),
             pltpu.VMEM((7, 8, dim), full),
             dma((5,)),
-            dma((7,)),
+            dma((3,)),
             dma((3,)),
             dma((3,)),
             dma((3, 2)),

time: 50.7 us -> 49.3 us (0.972)
  the two profiles are of different devices: /device:TPU:6 before, /device:TPU:71 now
where the time goes in v6:
time: 49.3 us; the launch traced here: 48.4 us
  Pallas kernels  47.7 us (97%)
  between operations  0.64 us (1%)
    pallas_call x1, Pallas kernels, per_device(): pl.pallas_call(kernel, out_shape=(jax.ShapeDtypeStruct((4, 2 * rows, dim)...  45.6 us
    pallas_call x1, Pallas kernels, per_device(): pl.pallas_call(place_kernel, out_shape=outs, in_specs=[vmem] * 4, out_spe...  2.08 us

profile of v6, /device:TPU:71, one launch (start us, length us, event | category | flops | bytes accessed | tf_op | source)
XLA Modules:
  0.0 48.4 jit_solution(8997251365971181105)
XLA Ops:
  0.6 45.6 %shard_map.102 = (bf16[4,288,128]{2,1,0:T(8,128)(2,1)}, f32[576,128]{1,0:T(8,128)}, f32[576,128]{1,0:T(8,128)}, f32[1,64]{1,0:T(1,128)}) custom-call(bf16[144,4096]{1,0:T(8,128)(2,1)} %q_ref.1, bf16[144,4096]{1,0:T(8,128)(2,1)} %g_ref.1, bf16[576,128]{1,0:T(8,128)(2,1)} %k_ref.1, bf16[576,128]{1,0:T(8,128)(2,1)} %v_ref.1, f32[32,64]{1,0:T(8,128)} %table_hbm.1, ...), custom_call_target="tpu_custom_call" | custom-call | flops 3397386240 | bytes 1179648 | tf_op jit(solution)/shard_map/pallas_call | solution.py:593
  46.3 2.1 %shard_map.103 = (f32[144,512]{1,0:T(8,128)}, f32[576,128]{1,0:T(8,128)}, f32[576,128]{1,0:T(8,128)}, f32[1,64]{1,0:T(1,128)}) custom-call(bf16[4,288,128]{2,1,0:T(8,128)(2,1)} %get-tuple-element.8.dq, f32[576,128]{1,0:T(8,128)} %get-tuple-element.9.dk, f32[576,128]{1,0:T(8,128)} %get-tuple-element.10.dv, f32[1,64]{1,0:T(1,128)} %get-tuple-element.11.db), custom_call_target="tpu_custom_call" | custom-call | tf_op jit(solution)/shard_map/pallas_call | solution.py:675

commit v7 on v6

--- a/solution.py
+++ b/solution.py
@@ -96,6 +96,8 @@
     state,
     stats,
     stats_got,
+    p_low,
+    ds_low,
     dq_all,
     held,
     dk_sum,
@@ -439,24 +441,24 @@
         best, total, moment = merge([stats[0:3, lo:hi], stats_got[0:3, lo:hi]])
         return best + jnp.log(total) * log2e, moment / total
 
-    def grads(c, b, lse, delta):
+    def score_grads(c, b, lse, delta):
         lo, hi = cuts[c], cuts[c + 1]
         part = slice(b * keys, (b + 1) * keys)
         p = jnp.exp2(s_all[part, lo:hi] - lse)
         ds = p * (dp_all[part, lo:hi] - delta)
         ds_lanes = sum(ds[:, n * dim : (n + 1) * dim] for n in range((hi - lo) // dim))
-        ds_low = ds.astype(jnp.bfloat16)
-        dv_part = nn_dot(p.astype(jnp.bfloat16), g_all[lo:hi, :])
-        dk_part = nn_dot(ds_low, q_all[lo:hi, :])
         if c == 0:
             ds_sum[part, :] = ds_lanes
-            dv_sum[part, :] = dv_part
-            dk_sum[part, :] = dk_part
         else:
             ds_sum[part, :] += ds_lanes
-            dv_sum[part, :] += dv_part
-            dk_sum[part, :] += dk_part
-        return nn_dot(k_turned[b], ds_low)
+        p_low[part, lo:hi] = p.astype(jnp.bfloat16)
+        ds_low[part, lo:hi] = ds.astype(jnp.bfloat16)
+        return nn_dot(k_turned[b], ds_low[part, lo:hi])
+
+    def key_grads(b):
+        part = slice(b * keys, (b + 1) * keys)
+        dk_sum[part, :] = nn_dot(ds_low[part, :], q_all[...])
+        dv_sum[part, :] = nn_dot(p_low[part, :], g_all[...])
 
     def send_dq(c, dq):
         dq_all[cuts[c] : cuts[c + 1], :] = (dq.T * scale).astype(jnp.bfloat16)
@@ -479,18 +481,23 @@
         kv_low[n] = low(total, b, factor)
         returns[n].start()
 
-    lse, delta = factors(0)
-    send_dq(0, sum(grads(0, b, lse, delta) for b in (2, 3, 1, 0)))
-    lse, delta = factors(1)
-    dq = grads(1, 2, lse, delta)
+    near = factors(0)
+    dq_near = score_grads(0, 2, *near)
+    rest = factors(1)
+    dq_rest = score_grads(1, 2, *rest)
+    key_grads(2)
     send_kv(0, dk_sum, 2, scale)
     send_kv(1, dv_sum, 2, 1.0)
-    dq = dq + grads(1, 3, lse, delta)
+    for b in (3, 1, 0):
+        dq_near = dq_near + score_grads(0, b, *near)
+    send_dq(0, dq_near)
+    for b in (3, 1, 0):
+        dq_rest = dq_rest + score_grads(1, b, *rest)
+    send_dq(1, dq_rest)
+    key_grads(3)
     send_kv(2, dk_sum, 3, scale)
-    dq = dq + grads(1, 1, lse, delta)
+    key_grads(1)
     send_kv(3, dv_sum, 1, 1.0)
-    send_dq(1, dq + grads(1, 0, lse, delta))
-
     column = jnp.sum(ds_sum[...], axis=1, keepdims=True)
     by_level = jnp.where(gap_cols[:, 0:levels] == level, column, 0.0)
     db_own[...] = jnp.zeros_like(db_own)
@@ -504,6 +511,8 @@
 
     for s in range(3):
         hand_on(s)
+    key_grads(0)
+
     returns[0].wait_recv()
     kv_low[4] = (dk_sum[keys : 2 * keys, :] * scale + kv_got[0].astype(jnp.float32)).astype(
         jnp.bfloat16
@@ -623,6 +632,8 @@
             pltpu.VMEM((3, 8, queries), full),
             pltpu.VMEM((8, queries), full),
             pltpu.VMEM((8, queries), full),
+            pltpu.VMEM((all_keys, queries), low),
+            pltpu.VMEM((all_keys, queries), low),
             pltpu.VMEM((queries, dim), low),
             pltpu.VMEM((slots, rows, dim), low),
             pltpu.VMEM((all_keys, dim), full),

time: 49.3 us -> 48.8 us (0.990)
  the two profiles are of different devices: /device:TPU:71 before, /device:TPU:8 now
where the time goes in v7:
time: 48.8 us; the launch traced here: 48.7 us
  Pallas kernels  48 us (98%)
  between operations  0.64 us (1%)
    pallas_call x1, Pallas kernels, per_device(): pl.pallas_call(kernel, out_shape=(jax.ShapeDtypeStruct((4, 2 * rows, dim)...  46 us
    pallas_call x1, Pallas kernels, per_device(): pl.pallas_call(place_kernel, out_shape=outs, in_specs=[vmem] * 4, out_spe...  2.08 us

profile of v7, /device:TPU:8, one launch (start us, length us, event | category | flops | bytes accessed | tf_op | source)
XLA Modules:
  0.0 48.7 jit_solution(12152553721486247710)
XLA Ops:
  0.6 46.0 %shard_map.102 = (bf16[4,288,128]{2,1,0:T(8,128)(2,1)}, f32[576,128]{1,0:T(8,128)}, f32[576,128]{1,0:T(8,128)}, f32[1,64]{1,0:T(1,128)}) custom-call(bf16[144,4096]{1,0:T(8,128)(2,1)} %q_ref.1, bf16[144,4096]{1,0:T(8,128)(2,1)} %g_ref.1, bf16[576,128]{1,0:T(8,128)(2,1)} %k_ref.1, bf16[576,128]{1,0:T(8,128)(2,1)} %v_ref.1, f32[32,64]{1,0:T(8,128)} %table_hbm.1, ...), custom_call_target="tpu_custom_call" | custom-call | flops 3397386240 | bytes 1179648 | tf_op jit(solution)/shard_map/pallas_call | solution.py:602
  46.6 2.1 %shard_map.103 = (f32[144,512]{1,0:T(8,128)}, f32[576,128]{1,0:T(8,128)}, f32[576,128]{1,0:T(8,128)}, f32[1,64]{1,0:T(1,128)}) custom-call(bf16[4,288,128]{2,1,0:T(8,128)(2,1)} %get-tuple-element.8.dq, f32[576,128]{1,0:T(8,128)} %get-tuple-element.9.dk, f32[576,128]{1,0:T(8,128)} %get-tuple-element.10.dv, f32[1,64]{1,0:T(1,128)} %get-tuple-element.11.db), custom_call_target="tpu_custom_call" | custom-call | tf_op jit(solution)/shard_map/pallas_call | solution.py:686
